TPU v7x, 256 devices: a whole 4x4x8 slice. The times are simulated.
256 devices in a mesh: blk: 32 (over y, z), head: 8 (over x, core).
Axes of the slice: x: 4, y: 4, z: 8, core: 2. Of those that a mesh axis runs over, the one named last changes fastest.
Arguments:
- queries: bfloat16 [24576, 64, 128], P(('blk', 'head')), may hold values from -6 to 6
- keys: bfloat16 [24576, 8, 128], P(('blk', 'head')), may hold values from -6 to 6
- values: bfloat16 [24576, 8, 128], P(('blk', 'head')), may hold values from -6 to 6
- out_grad: bfloat16 [24576, 64, 128], P(('blk', 'head')), may hold values from -6 to 6
- rand_blocks: int32 [192, 8, 3], replicated, may hold values from 0 to 191, as said below
- global_blocks: int32 [2], replicated, may hold values from 0 to 191
Outputs:
- attn_out: bfloat16 [24576, 64, 128], P(('blk', 'head'))
- query_grad: bfloat16 [24576, 64, 128], P(('blk', 'head'))
- key_grad: bfloat16 [24576, 8, 128], P(('blk', 'head'))
- value_grad: bfloat16 [24576, 8, 128], P(('blk', 'head'))
Inputs may be any that keep to these rules, and one draw needn't show every extreme that they name: `rand_blocks`: for every shard of 6 query blocks and every KV head, the 18 random entries name blocks of any one shard at most 1 times, and some shard exactly 1 times.
All inputs are finite; a program needn't handle non-finite values.
Results may differ from a plain program's by a relative error of at most 0.02.
Values may be sent and summed in bfloat16 or wider, within the bound.
A program may use at most 128 MiB of HBM per device.

v0:
```python
import math

import jax
import jax.numpy as jnp
from jax import lax
from jax.sharding import PartitionSpec as P


def attend_rows(query_blk, key_blk, value_blk, grad_blk, scaling):
    scores = (
        jnp.einsum("tgad,gkd->gatk", query_blk, key_blk, preferred_element_type=jnp.float32)
        * scaling
    )
    peak = jnp.max(scores, axis=-1, keepdims=True)
    expo = jnp.exp(scores - peak)
    probs = expo / jnp.sum(expo, axis=-1, keepdims=True)
    probs_b = probs.astype(jnp.bfloat16)
    output = jnp.einsum(
        "gatk,gkd->tgad", probs_b, value_blk, preferred_element_type=jnp.float32
    ).astype(jnp.bfloat16)
    delta = jnp.einsum("tgad,tgad->gat", output, grad_blk, preferred_element_type=jnp.float32)[
        ..., None
    ]
    dprobs = jnp.einsum("tgad,gkd->gatk", grad_blk, value_blk, preferred_element_type=jnp.float32)
    dscores = (probs * (dprobs - delta)).astype(jnp.bfloat16)
    query_grad = (
        jnp.einsum("gatk,gkd->tgad", dscores, key_blk, preferred_element_type=jnp.float32) * scaling
    ).astype(jnp.bfloat16)
    key_terms = (
        jnp.einsum("gatk,tgad->gkd", dscores, query_blk, preferred_element_type=jnp.float32)
        * scaling
    )
    value_terms = jnp.einsum(
        "gatk,tgad->gkd", probs_b, grad_blk, preferred_element_type=jnp.float32
    )
    return (output, query_grad, key_terms, value_terms)


def assemble(local_blocks, slot_blocks, blocks_here, random_count):
    kv_local = local_blocks.shape[0]
    tail = slot_blocks.shape[2:]
    extended = jnp.concatenate([slot_blocks[:, 0:1], local_blocks, slot_blocks[:, 1:2]], axis=1)
    window_part = jnp.stack(
        [extended[:, offset : offset + blocks_here] for offset in range(3)], axis=2
    )
    global_part = jnp.broadcast_to(slot_blocks[:, None, 2:4], (kv_local, blocks_here, 2) + tail)
    random_part = slot_blocks[:, 4:].reshape((kv_local, blocks_here, random_count) + tail)
    joined = jnp.concatenate([window_part, global_part, random_part], axis=2)
    return joined.reshape(kv_local, blocks_here, -1, tail[-1]).transpose(1, 0, 2, 3)


def spread(parts, blocks_here, block_len, random_count):
    kv_local = parts.shape[1]
    head_dim = parts.shape[-1]
    parts = parts.reshape(blocks_here, kv_local, 5 + random_count, block_len, head_dim)
    moved = parts.transpose(1, 0, 2, 3, 4)
    extended = jnp.zeros((kv_local, blocks_here + 2, block_len, head_dim), jnp.float32)
    for offset in range(3):
        extended = extended.at[:, offset : offset + blocks_here].add(moved[:, :, offset])
    local_sum = extended[:, 1 : blocks_here + 1]
    edge_sum = jnp.stack([extended[:, 0], extended[:, blocks_here + 1]], axis=1)
    global_sum = jnp.sum(moved[:, :, 3:5], axis=1)
    random_sum = moved[:, :, 5:].reshape(kv_local, blocks_here * random_count, block_len, head_dim)
    return (local_sum, jnp.concatenate([edge_sum, global_sum, random_sum], axis=1))


def slot_table(rand_blocks, global_blocks, head_start, kv_local, shard_count, blocks_here):
    total_blocks = shard_count * blocks_here
    random_count = rand_blocks.shape[2]
    targets = jnp.arange(shard_count, dtype=jnp.int32)
    left_edge = (targets * blocks_here - 1) % total_blocks
    right_edge = (targets * blocks_here + blocks_here) % total_blocks
    edges = jnp.stack([left_edge, right_edge], axis=1)[:, None, :]
    global_here = jnp.broadcast_to(global_blocks[None, None, :], (shard_count, kv_local, 2))
    chosen = lax.dynamic_slice_in_dim(rand_blocks, head_start, kv_local, 1)
    chosen = chosen.reshape(shard_count, blocks_here, kv_local, random_count).transpose(0, 2, 1, 3)
    chosen = chosen.reshape(shard_count, kv_local, blocks_here * random_count)
    return jnp.concatenate([edges, global_here, chosen], axis=2)


def slot_ranks(owners, shard_count):
    onehot = (owners[..., None] == jnp.arange(shard_count, dtype=jnp.int32)).astype(jnp.int32)
    before = jnp.cumsum(onehot, axis=2) - onehot
    return jnp.sum(before * onehot, axis=3)


def routing(table, shard_index, shard_count, blocks_here, capacity):
    owners = table // blocks_here
    within = table % blocks_here
    ranks = slot_ranks(owners, shard_count)
    positions = jnp.arange(capacity, dtype=jnp.int32)
    matches = (owners == shard_index)[..., None] & (ranks[..., None] == positions)
    send_local = jnp.sum(jnp.where(matches, within[..., None], 0), axis=2)
    send_valid = jnp.any(matches, axis=2)
    return (send_local, send_valid, owners[shard_index], ranks[shard_index], positions)


def pack_slots(slot_part, my_owner, my_rank, positions, shard_count):
    owner_hit = my_owner[:, :, None, None] == jnp.arange(shard_count, dtype=jnp.int32)[:, None]
    rank_hit = my_rank[:, :, None, None] == positions
    placing = (owner_hit & rank_hit).astype(jnp.bfloat16)
    return jnp.einsum(
        "gsoc,gstd->ogctd", placing, slot_part, preferred_element_type=jnp.float32
    ).astype(jnp.bfloat16)


def unpack_slots(back, send_local, send_valid, blocks_here):
    select = (
        send_valid[..., None] & (send_local[..., None] == jnp.arange(blocks_here, dtype=jnp.int32))
    ).astype(jnp.bfloat16)
    return jnp.einsum("ogcb,ogctd->gbtd", select, back, preferred_element_type=jnp.float32)


def on_device(queries, keys, values, out_grad, rand_blocks, global_blocks):
    shard_count = lax.axis_size("blk")
    shard_index = lax.axis_index("blk")
    head_index = lax.axis_index("head")
    query_h, key_h, value_h, grad_h = (
        lax.all_to_all(queries, "head", split_axis=1, concat_axis=0, tiled=True),
        lax.all_to_all(keys, "head", split_axis=1, concat_axis=0, tiled=True),
        lax.all_to_all(values, "head", split_axis=1, concat_axis=0, tiled=True),
        lax.all_to_all(out_grad, "head", split_axis=1, concat_axis=0, tiled=True),
    )
    seq_rows, heads_local, head_dim = query_h.shape
    kv_local = key_h.shape[1]
    group = heads_local // kv_local
    blocks_here = rand_blocks.shape[0] // shard_count
    block_len = seq_rows // blocks_here
    random_count = rand_blocks.shape[2]
    rand_capacity = (blocks_here * random_count + shard_count - 1) // shard_count
    capacity = rand_capacity + 3
    scaling = 1.0 / math.sqrt(head_dim)
    table = slot_table(
        rand_blocks, global_blocks, head_index * kv_local, kv_local, shard_count, blocks_here
    )
    send_local, send_valid, my_owner, my_rank, positions = routing(
        table, shard_index, shard_count, blocks_here, capacity
    )
    my_ids = table[shard_index]
    key_blocks = key_h.reshape(blocks_here, block_len, kv_local, head_dim).transpose(2, 0, 1, 3)
    value_blocks = value_h.reshape(blocks_here, block_len, kv_local, head_dim).transpose(2, 0, 1, 3)
    cycle_keys = key_h.reshape(blocks_here, block_len, kv_local, head_dim).transpose(0, 2, 1, 3)
    cycle_values = value_h.reshape(blocks_here, block_len, kv_local, head_dim).transpose(0, 2, 1, 3)
    pieces = (
        lax.all_gather(cycle_keys, "blk", axis=0, tiled=True),
        lax.all_gather(cycle_values, "blk", axis=0, tiled=True),
    )
    count = pieces[0].shape[0]
    pick = (my_ids[..., None] == jnp.arange(count, dtype=jnp.int32)).astype(jnp.bfloat16)
    new_keys = jnp.einsum("gsn,ngtd->gstd", pick, pieces[0], preferred_element_type=jnp.float32)
    new_values = jnp.einsum("gsn,ngtd->gstd", pick, pieces[1], preferred_element_type=jnp.float32)
    slot_keys = new_keys.astype(jnp.bfloat16)
    slot_values = new_values.astype(jnp.bfloat16)
    key_sets = assemble(key_blocks, slot_keys, blocks_here, random_count)
    value_sets = assemble(value_blocks, slot_values, blocks_here, random_count)
    query_steps = query_h.reshape(blocks_here, block_len, kv_local, group, head_dim)
    grad_steps = grad_h.reshape(blocks_here, block_len, kv_local, group, head_dim)

    def step_block(carry, inputs):
        return (carry, attend_rows(inputs[0], inputs[1], inputs[2], inputs[3], scaling))

    unused, results = lax.scan(
        step_block, jnp.int32(0), (query_steps, key_sets, value_sets, grad_steps)
    )
    out_blocks, dq_blocks, key_terms, value_terms = results
    local_k, slot_k = spread(key_terms, blocks_here, block_len, random_count)
    local_v, slot_v = spread(value_terms, blocks_here, block_len, random_count)
    slot_kb = slot_k.astype(jnp.bfloat16)
    slot_vb = slot_v.astype(jnp.bfloat16)
    pack_k = pack_slots(slot_kb, my_owner, my_rank, positions, shard_count)
    pack_v = pack_slots(slot_vb, my_owner, my_rank, positions, shard_count)
    back_k, back_v = (
        lax.all_to_all(pack_k, "blk", split_axis=0, concat_axis=0, tiled=True),
        lax.all_to_all(pack_v, "blk", split_axis=0, concat_axis=0, tiled=True),
    )
    added_k = unpack_slots(back_k, send_local, send_valid, blocks_here)
    added_v = unpack_slots(back_v, send_local, send_valid, blocks_here)
    total_k = (local_k + added_k).astype(jnp.bfloat16)
    total_v = (local_v + added_v).astype(jnp.bfloat16)
    out_rows = out_blocks.reshape(seq_rows, heads_local, head_dim)
    dq_rows = dq_blocks.reshape(seq_rows, heads_local, head_dim)
    dk_rows = total_k.transpose(1, 2, 0, 3).reshape(seq_rows, kv_local, head_dim)
    dv_rows = total_v.transpose(1, 2, 0, 3).reshape(seq_rows, kv_local, head_dim)
    attn_out, query_grad, key_grad, value_grad = (
        lax.all_to_all(out_rows, "head", split_axis=0, concat_axis=1, tiled=True),
        lax.all_to_all(dq_rows, "head", split_axis=0, concat_axis=1, tiled=True),
        lax.all_to_all(dk_rows, "head", split_axis=0, concat_axis=1, tiled=True),
        lax.all_to_all(dv_rows, "head", split_axis=0, concat_axis=1, tiled=True),
    )
    return (attn_out, query_grad, key_grad, value_grad)


def solution(mesh):
    return jax.shard_map(
        on_device,
        mesh=mesh,
        in_specs=(
            P(("blk", "head"), None, None),
            P(("blk", "head"), None, None),
            P(("blk", "head"), None, None),
            P(("blk", "head"), None, None),
            P(),
            P(),
        ),
        out_specs=(
            P(("blk", "head"), None, None),
            P(("blk", "head"), None, None),
            P(("blk", "head"), None, None),
            P(("blk", "head"), None, None),
        ),
        check_vma=False,
    )
```

profile of v0, /device:TPU:1, one launch (start us, length us, event | category | flops | bytes accessed | tf_op | source)
XLA Modules:
  0.0 607.3 jit_solution(13134746731719926146)
XLA Ops:
  8.3 12.2 %all_to_all.142 = bf16[96,8,128]{2,0,1:T(8,128)(2,1)} all-to-all(bf16[96,8,128]{2,0,1:T(8,128)(2,1)S(1)} %copy.392), channel_id=1, replica_groups=mesh['blk'=32,'head'=8] {'head'}, dimensions={1} | all-to-all | bytes 393216 | tf_op jit(solution)/shard_map/all_to_all | solution.py:121
  21.5 9.9 %all_to_all.143 = bf16[96,8,128]{2,0,1:T(8,128)(2,1)} all-to-all(bf16[96,8,128]{2,0,1:T(8,128)(2,1)S(1)} %copy.402), channel_id=1, replica_groups=mesh['blk'=32,'head'=8] {'head'}, dimensions={1} | all-to-all | bytes 393216 | tf_op jit(solution)/shard_map/all_to_all | solution.py:120
  31.5 2.2 copy.412
  33.6 4.6 all-to-all-start.2
  38.2 2.2 copy.415
  40.4 18.6 %all-to-all-done.2 = bf16[96,64,128]{2,0,1:T(8,128)(2,1)S(1)} async-done(((bf16[96,64,128]{2,0,1:T(8,128)(2,1)}), bf16[96,64,128]{2,0,1:T(8,128)(2,1)S(1)}, u32[]{:S(2)}, u32[]{:S(2)}) %all-to-all-start.2) | async-done | bytes 1572896 | tf_op jit(solution)/shard_map/all_to_all | solution.py:119
  58.9 5.0 all-to-all-start.3
  64.5 1.8 copy.414
  66.3 18.3 %all-to-all-done.3 = bf16[96,64,128]{2,0,1:T(8,128)(2,1)S(1)} async-done(((bf16[96,64,128]{2,0,1:T(8,128)(2,1)}), bf16[96,64,128]{2,0,1:T(8,128)(2,1)S(1)}, u32[]{:S(2)}, u32[]{:S(2)}) %all-to-all-start.3) | async-done | bytes 1572896 | tf_op jit(solution)/shard_map/all_to_all | solution.py:122
  84.6 1.8 copy.417
  86.4 23.5 %all-gather.3.cloned.1.call-done = bf16[192,1,128,128]{3,2,1,0:T(8,128)(2,1)} async-done(((bf16[6,1,128,128]{3,2,1,0:T(8,128)(2,1)}), bf16[192,1,128,128]{3,2,1,0:T(8,128)(2,1)}) %all-gather.3.cloned.1.call-update) | async-done | bytes 6291472 | tf_op jit(solution)/shard_map/all_gather | solution.py:146
  109.8 6.3 %fusion.86 = bf16[1,22,128,128]{3,1,2,0:T(8,128)(2,1)S(1)} fusion(bf16[192,1,128,128]{3,2,1,0:T(8,128)(2,1)} %all-gather.3.cloned.1.call-done, s32[22]{0:T(128)S(1)} %get-tuple-element.258), kind=kOutput, calls=%fused_computation.72 | convolution fusion | flops 138776704 | bytes 7012440 | tf_op jit(solution)/shard_map/gsn,ngtd->gstd/dot_general | solution.py:151
  116.7 81.4 %all-gather.5.cloned.1.call-done = bf16[192,1,128,128]{3,2,1,0:T(8,128)(2,1)} async-done(((bf16[6,1,128,128]{3,2,1,0:T(8,128)(2,1)}), bf16[192,1,128,128]{3,2,1,0:T(8,128)(2,1)}) %all-gather.5.cloned.1.call-update) | async-done | bytes 6291472 | tf_op jit(solution)/shard_map/all_gather | solution.py:145
  198.1 6.3 %fusion.83 = bf16[1,22,128,128]{3,1,2,0:T(8,128)(2,1)S(1)} fusion(bf16[192,1,128,128]{3,2,1,0:T(8,128)(2,1)} %all-gather.5.cloned.1.call-done, s32[22]{0:T(128)S(1)} %get-tuple-element.258), kind=kOutput, calls=%fused_computation.71 | convolution fusion | flops 138776704 | bytes 7012440 | tf_op jit(solution)/shard_map/gsn,ngtd->gstd/dot_general | solution.py:150
  213.7 98.6 %while.22 = (s32[]{:T(128)}, bf16[6,128,1,8,128]{4,3,1,0,2:T(8,128)(2,1)}, bf16[6,128,1,8,128]{4,3,1,0,2:T(8,128)(2,1)}, f32[6,1,1024,128]{3,2,1,0:T(8,128)}, f3...) while((s32[]{:T(128)}, ...), condition=%wide.region_3.4_spmd, body=%wide.region_0.3_spmd.sunk | while | flops 1631581184 | bytes 53264008 | solution.py:162
  214.8 1.7 bitcast_reduce_fusion.2
  218.4 1.7 fusion.192
  220.1 2.0 bitcast_convert_fusion.2
  222.5 3.5 fusion.189
  231.2 1.7 bitcast_reduce_fusion.2
  234.8 1.7 fusion.192
  236.5 2.0 bitcast_convert_fusion.2
  238.9 3.5 fusion.189
  247.6 1.7 bitcast_reduce_fusion.2
  251.2 1.7 fusion.192
  252.9 2.0 bitcast_convert_fusion.2
  255.4 3.5 fusion.189
  264.0 1.7 bitcast_reduce_fusion.2
  267.6 1.7 fusion.192
  269.3 2.0 bitcast_convert_fusion.2
  271.7 3.5 fusion.189
  280.4 1.7 bitcast_reduce_fusion.2
  284.0 1.7 fusion.192
  285.7 2.0 bitcast_convert_fusion.2
  288.1 3.5 fusion.189
  296.8 1.7 bitcast_reduce_fusion.2
  300.4 1.7 fusion.192
  302.1 2.0 bitcast_convert_fusion.2
  304.5 3.5 fusion.189
  312.2 5.3 all-to-all-start.5
  318.8 19.4 %all-to-all-done.5 = bf16[768,8,128]{2,1,0:T(8,128)(2,1)S(1)} async-done(((bf16[768,8,128]{2,1,0:T(8,128)(2,1)}), bf16[768,8,128]{2,1,0:T(8,128)(2,1)S(1)}, u32[]{:S(2)}, u32[]{:S(2)}) %all-to-all-start.5) | async-done | bytes 1572896 | tf_op jit(solution)/shard_map/all_to_all | solution.py:186
  338.3 4.6 all-to-all-start.4
  342.9 2.1 fusion.164
  351.0 4.1 scatter-add.26
  355.1 2.2 slice_add_fusion
  357.3 4.1 scatter-add.29
  363.7 2.5 convert_bitcast_fusion
  366.2 4.1 copy.446
  370.3 5.6 all-to-all-start.8
  375.9 2.2 slice.347
  378.1 2.1 fusion.165
  382.4 4.1 scatter-add.21
  386.6 2.2 slice_add_fusion.1
  388.8 4.1 scatter-add.24
  399.2 4.1 copy.435
  403.4 67.1 %all-to-all-done.8 = bf16[32,1,4,128,128]{4,2,3,1,0:T(4,128)(2,1)} async-done(((bf16[32,1,4,128,128]{4,2,3,1,0:T(4,128)(2,1)}), bf16[32,1,4,128,128]{4,2,3,1,0:T(4,128)(2,1)}, u32[]{:S(2)}, u32[]{:S(2)}) %all-to-all-start.8) | async-done | bytes 4194336 | tf_op jit(solution)/shard_map/all_to_all | solution.py:174
  470.4 7.7 %all-to-all-start.6 = ((bf16[32,1,4,128,128]{4,2,3,1,0:T(4,128)(2,1)}), bf16[32,1,4,128,128]{4,2,3,1,0:T(4,128)(2,1)}, u32[]{:S(2)}, u32[]{:S(2)}) async-start(bf16[32,1,4,128,128]{4,2,3,1,0:T(4,128)(2,1)} %copy.435), calls=%async_computation.6 | async-start | bytes 8388608 | tf_op jit(solution)/shard_map/all_to_all | solution.py:173
  478.3 4.7 fusion.105
  484.9 1.7 reshape.1047
  486.6 85.4 %all-to-all-done.6 = bf16[32,1,4,128,128]{4,2,3,1,0:T(4,128)(2,1)} async-done(((bf16[32,1,4,128,128]{4,2,3,1,0:T(4,128)(2,1)}), bf16[32,1,4,128,128]{4,2,3,1,0:T(4,128)(2,1)}, u32[]{:S(2)}, u32[]{:S(2)}) %all-to-all-start.6) | async-done | bytes 4194336 | tf_op jit(solution)/shard_map/all_to_all | solution.py:173
  572.0 8.7 %all-to-all-start.9 = ((bf16[8,2,6144]{2,1,0:T(2,128)(2,1)}), bf16[8,2,6144]{2,1,0:T(2,128)(2,1)}, u32[]{:S(2)}, u32[]{:S(2)}) async-start(bf16[8,2,6144]{2,1,0:T(2,128)(2,1)} %reshape.1047), calls=%async_computation.9 | async-start | bytes 393216 | tf_op jit(solution)/shard_map/all_to_all | solution.py:188
  580.7 4.7 fusion.102
  586.8 1.7 reshape.1045
  588.5 4.8 all-to-all-start.7
  (173 shorter events, 85.2 us)
Async XLA Ops:
  7.2 56.8 %copy-start = (s32[192,8,3]{0,1,2:T(8,128)S(1)}, s32[192,8,3]{0,1,2:T(8,128)}, u32[]{:S(2)}) copy-start(s32[192,8,3]{0,1,2:T(8,128)} %param.24) | copy-start | bytes 55300
  7.2 24.3 %copy-start.5 = (bf16[96,64,128]{2,1,0:T(8,128)(2,1)S(1)}, bf16[96,64,128]{2,1,0:T(8,128)(2,1)}, u32[]{:S(2)}) copy-start(bf16[96,64,128]{2,1,0:T(8,128)(2,1)} %param.20) | copy-start | bytes 4718596
  7.2 102.6 %all-gather.3.cloned.1.call-start = ((), (), s32[]{:S(2)}) async-start(), calls=%async_computation.10 | async-start | bytes 6488064 | tf_op jit(solution)/shard_map/all_gather | solution.py:146
  20.5 177.6 %all-gather.5.cloned.1.call-start = ((), (), s32[]{:S(2)}) async-start(), calls=%async_computation.11 | async-start | bytes 6488064 | tf_op jit(solution)/shard_map/all_gather | solution.py:145
  33.6 4.6 copy-start.6
  33.6 25.3 %all-to-all-start.2 = ((bf16[96,64,128]{2,0,1:T(8,128)(2,1)}), bf16[96,64,128]{2,0,1:T(8,128)(2,1)S(1)}, u32[]{:S(2)}, u32[]{:S(2)}) async-start(bf16[96,64,128]{2,0,1:T(8,128)(2,1)} %copy.412), calls=%async_computation.2 | async-start | bytes 3145728 | tf_op jit(solution)/shard_map/all_to_all | solution.py:119
  40.4 24.0 %copy-start.7 = (s32[2]{0:T(128)S(1)}, s32[2]{0:T(128)}, u32[]{:S(2)}) copy-start(s32[2]{0:T(128)} %param.25) | copy-start | bytes 28
  58.9 25.7 %all-to-all-start.3 = ((bf16[96,64,128]{2,0,1:T(8,128)(2,1)}), bf16[96,64,128]{2,0,1:T(8,128)(2,1)S(1)}, u32[]{:S(2)}, u32[]{:S(2)}) async-start(bf16[96,64,128]{2,0,1:T(8,128)(2,1)} %copy.415), calls=%async_computation.3 | async-start | bytes 3145728 | tf_op jit(solution)/shard_map/all_to_all | solution.py:122
  204.9 0.9 copy-start.4
  205.2 4.6 copy-start.3
  216.5 3.6 copy-start.2
  232.9 3.6 copy-start.2
  249.3 3.6 copy-start.2
  265.7 3.6 copy-start.2
  282.1 3.6 copy-start.2
  298.5 3.6 copy-start.2
  312.2 26.0 %all-to-all-start.5 = ((bf16[768,8,128]{2,1,0:T(8,128)(2,1)}), bf16[768,8,128]{2,1,0:T(8,128)(2,1)S(1)}, u32[]{:S(2)}, u32[]{:S(2)}) async-start(bf16[768,8,128]{2,1,0:T(8,128)(2,1)} %bitcast.434), calls=%async_computation.5 | async-start | bytes 3145728 | tf_op jit(solution)/shard_map/all_to_all | solution.py:186
  338.3 32.0 %all-to-all-start.4 = ((bf16[768,8,128]{2,1,0:T(8,128)(2,1)}), bf16[768,8,128]{2,1,0:T(8,128)(2,1)S(1)}, u32[]{:S(2)}, u32[]{:S(2)}) async-start(bf16[768,8,128]{2,1,0:T(8,128)(2,1)} %bitcast.433), calls=%async_computation.4 | async-start | bytes 3145728 | tf_op jit(solution)/shard_map/all_to_all | solution.py:185
  370.3 100.1 %all-to-all-start.8 = ((bf16[32,1,4,128,128]{4,2,3,1,0:T(4,128)(2,1)}), bf16[32,1,4,128,128]{4,2,3,1,0:T(4,128)(2,1)}, u32[]{:S(2)}, u32[]{:S(2)}) async-start(bf16[32,1,4,128,128]{4,2,3,1,0:T(4,128)(2,1)} %copy.446), calls=%async_computation.8 | async-start | bytes 8388608 | tf_op jit(solution)/shard_map/all_to_all | solution.py:174
  470.4 101.6 %all-to-all-start.6 = ((bf16[32,1,4,128,128]{4,2,3,1,0:T(4,128)(2,1)}), bf16[32,1,4,128,128]{4,2,3,1,0:T(4,128)(2,1)}, u32[]{:S(2)}, u32[]{:S(2)}) async-start(bf16[32,1,4,128,128]{4,2,3,1,0:T(4,128)(2,1)} %copy.435), calls=%async_computation.6 | async-start | bytes 8388608 | tf_op jit(solution)/shard_map/all_to_all | solution.py:173
  572.0 16.5 %all-to-all-start.9 = ((bf16[8,2,6144]{2,1,0:T(2,128)(2,1)}), bf16[8,2,6144]{2,1,0:T(2,128)(2,1)}, u32[]{:S(2)}, u32[]{:S(2)}) async-start(bf16[8,2,6144]{2,1,0:T(2,128)(2,1)} %reshape.1047), calls=%async_computation.9 | async-start | bytes 393216 | tf_op jit(solution)/shard_map/all_to_all | solution.py:188
  588.5 10.7 %all-to-all-start.7 = ((bf16[8,2,6144]{2,1,0:T(2,128)(2,1)}), bf16[8,2,6144]{2,1,0:T(2,128)(2,1)S(1)}, u32[]{:S(2)}, u32[]{:S(2)}) async-start(bf16[8,2,6144]{2,1,0:T(2,128)(2,1)} %reshape.1045), calls=%async_computation.7 | async-start | bytes 393216 | tf_op jit(solution)/shard_map/all_to_all | solution.py:187
  594.9 5.3 copy-start.1
Sparse Core Ops, SparseCore 0:
  20.6 89.1 all-gather.2
  112.4 85.6 all-gather.4
where the time goes:
time: 613 us; the launch traced here: 607 us
  waiting for transfers between devices  314 us (51%)
  matrix products  97 us (16%)
  local copies, waits for them, and re-layouts  91.3 us (15%)
  starting transfers between devices  46.3 us (8%)
  blocking collectives  22.1 us (4%)
  other arithmetic  21.2 us (3%)
  between operations  14.8 us (2%)
    all_to_all x1, waiting for transfers between devices, on_device(): lax.all_to_all(pack_k, 'blk', split_axis=0, concat_axis=0, tiled=True)  85.4 us
    all_gather x1, waiting for transfers between devices, on_device(): lax.all_gather(cycle_keys, 'blk', axis=0, tiled=True)  81.4 us
    all_to_all x1, waiting for transfers between devices, on_device(): lax.all_to_all(pack_v, 'blk', split_axis=0, concat_axis=0, tiled=True)  67.1 us
    all_gather x1, waiting for transfers between devices, on_device(): lax.all_gather(cycle_values, 'blk', axis=0, tiled=True)  23.5 us
    dot_general x6, matrix products, attend_rows(): jnp.einsum('tgad,gkd->gatk', grad_blk, value_blk, preferred_element_type=...  21.1 us
    all_to_all x1, waiting for transfers between devices, on_device(): lax.all_to_all(dq_rows, 'head', split_axis=0, concat_axis=1, tiled=True)  19.4 us
    all_to_all x1, waiting for transfers between devices, on_device(): lax.all_to_all(queries, 'head', split_axis=1, concat_axis=0, tiled=True)  18.6 us
    all_to_all x1, waiting for transfers between devices, on_device(): lax.all_to_all(out_grad, 'head', split_axis=1, concat_axis=0, tiled=True)  18.3 us
  transfers between devices with their start and end apart: 10, of which 8 were waited for; matrix products, arithmetic and copies ran while one was open for 15% of the time, Pallas kernels for 0%

commit v1 on v0

v1 whole, which is shorter than its diff:
```python
import functools
import math

import jax
import jax.numpy as jnp
from jax import lax
from jax.experimental import pallas as pl
from jax.experimental.pallas import tpu as pltpu
from jax.sharding import PartitionSpec as P

MESH = pl.DeviceIdType.MESH
NY, NZ, NH = 4, 8, 8
QB, BS, DH, RAND = 6, 128, 128, 3
ROWS = QB * BS
PART = ROWS // NH
LIST = 8 * BS
CHUNK = 256
SLOTS = QB * RAND
SCALE = 1.0 / math.sqrt(DH)
LOG2E = 1.4426950408889634
F32, BF16 = jnp.float32, jnp.bfloat16

T_WANT, T_PICK, T_OWN, T_SLOT, T_GLOB = 0, 32, 64, 82, 114


def dot(a, b, dims):
    return lax.dot_general(a, b, (dims, ((), ())), preferred_element_type=F32)


def flag(a, b):
    return (a == b).astype(jnp.int32).astype(F32)


def body(
    tab, q_s, g_s, kv_s, o_out, dq_out, dkv_out,
    qh, gh, r0, rp1, rp2, rp3, rm1, rm2, rm3, r4, xs, xr, edge, gs, gr,
    lk, lv, lkt, lvt, ob, dqb, awk, awv, agk, agv, ark, arv,
    ys, yr, es, er, gs2, gr2, part, ssp, ssm, srp, srm, dkvb,
    head_ss, head_rs, q_ss, q_rs, g_ss, g_rs, loc,
    zp_ss, zp_rs, zm_ss, zm_rs, e_ss, e_rs, y_ss, y_rs, gl_ss, gl_rs,
    o_ss, o_rs, dq_ss, dq_rs, w_ss, w_rs, e2_ss, e2_rs, gl2_ss, gl2_rs,
    pp_ss, pp_rs, pm_ss, pm_rs, dkv_ss, dkv_rs,
):
    blk = lax.axis_index("blk")
    head = lax.axis_index("head")
    y, z = blk // NZ, blk % NZ
    x = head // 2
    up = (y * NZ + (z + 1) % NZ, head)
    down = (y * NZ + (z + NZ - 1) % NZ, head)
    after = ((blk + 1) % (NY * NZ), head)
    before = ((blk + NY * NZ - 1) % (NY * NZ), head)

    def column(dy):
        return (((y + dy) % NY) * NZ + z, head)

    def remote(src, dst, ss, rs, dev):
        return pltpu.make_async_remote_copy(
            src_ref=src, dst_ref=dst, send_sem=ss, recv_sem=rs, device_id=dev, device_id_type=MESH
        )

    bar = pltpu.get_barrier_semaphore()

    def greet(dev):
        pl.semaphore_signal(bar, inc=1, device_id=dev, device_id_type=MESH)

    def greet_head(k, c):
        greet((blk, (head + k) % NH))
        return c

    lax.fori_loop(1, NH, greet_head, 0)
    for dev in (up, down, after, before):
        greet(dev)
    for dy in range(1, NY):
        greet(column(dy))
    pl.semaphore_wait(bar, NH - 1 + 4 + NY - 1)

    mine = pl.ds(pl.multiple_of(head * PART, 32), PART)
    rows_mine = pl.ds(pl.multiple_of(head * ROWS, 256), ROWS)

    def kv_copy(h):
        return remote(kv_s.at[h], r0.at[:, mine, :], head_ss.at[h], head_rs.at[head], (blk, h))

    def kv_arrival(h):
        there = pl.ds(pl.multiple_of(h * PART, 32), PART)
        return remote(kv_s.at[h], r0.at[:, there, :], head_ss.at[h], head_rs.at[h], (blk, h))

    def q_copy(h):
        return remote(q_s.at[h], qh.at[rows_mine, :], q_ss.at[h], q_rs.at[head], (blk, h))

    def g_copy(h):
        return remote(g_s.at[h], gh.at[rows_mine, :], g_ss.at[h], g_rs.at[head], (blk, h))

    def q_arrival(h):
        there = pl.ds(pl.multiple_of(h * ROWS, 256), ROWS)
        return remote(q_s.at[h], qh.at[there, :], q_ss.at[h], q_rs.at[h], (blk, h))

    def g_arrival(h):
        there = pl.ds(pl.multiple_of(h * ROWS, 256), ROWS)
        return remote(g_s.at[h], gh.at[there, :], g_ss.at[h], g_rs.at[h], (blk, h))

    own_kv = pltpu.make_async_copy(kv_s.at[head], r0.at[:, mine, :], loc.at[0])
    own_q = pltpu.make_async_copy(q_s.at[head], qh.at[rows_mine, :], loc.at[1])
    own_g = pltpu.make_async_copy(g_s.at[head], gh.at[rows_mine, :], loc.at[2])
    own_kv.start()

    def send_kv(k, c):
        kv_copy((head + k) % NH).start()
        return c

    def send_qg(k, c):
        h = (head + k) % NH
        q_copy(h).start()
        g_copy(h).start()
        return c

    lax.fori_loop(1, NH, send_kv, 0)
    own_q.start()
    own_g.start()
    lax.fori_loop(1, NH, send_qg, 0)

    zero = jnp.zeros((BS, DH), F32)
    for ref in (awk, awv, agk, agv, ark, arv):
        def clear(n, c, ref=ref):
            ref[pl.ds(pl.multiple_of(n * BS, BS), BS), :] = zero
            return c
        lax.fori_loop(0, ref.shape[0] // BS, clear, 0)

    own_kv.wait()

    def wait_kv(k, c):
        kv_arrival((head + k) % NH).wait_recv()
        return c

    lax.fori_loop(1, NH, wait_kv, 0)

    plus = [r0, rp1, rp2, rp3, r4]
    minus = [r0, rm1, rm2, rm3, r4]

    def z_copy(step, half, upward):
        chain = plus if upward else minus
        ss, rs = (zp_ss, zp_rs) if upward else (zm_ss, zm_rs)
        return remote(
            chain[step].at[half], chain[step + 1].at[half],
            ss.at[step, half], rs.at[step, half], up if upward else down,
        )

    to_after = remote(r0.at[:, pl.ds(ROWS - BS, BS), :], edge.at[0], e_ss.at[0], e_rs.at[0], after)
    to_before = remote(r0.at[:, pl.ds(0, BS), :], edge.at[1], e_ss.at[1], e_rs.at[1], before)
    for half in (0, 1):
        z_copy(0, half, True).start()
        z_copy(0, half, False).start()
    to_after.start()
    to_before.start()

    glob = [tab[T_GLOB + j] for j in range(2)]
    g_within = [tab[T_GLOB + 2 + j] for j in range(2)]
    g_z = [tab[T_GLOB + 4 + j] for j in range(2)]
    g_y = [tab[T_GLOB + 6 + j] for j in range(2)]

    def block_rows(w):
        return pl.ds(w * BS, BS)

    def y_copy(dy, index, shard_z):
        dev = column(dy)
        return remote(
            xs.at[index * 4 + dy], xr.at[y * NZ + shard_z],
            y_ss.at[index, dy], y_rs.at[index, (NY - dy) % NY], dev,
        )

    def y_arrival(dy, index, shard_z):
        return remote(
            xs.at[index * 4 + dy], xr.at[((y + dy) % NY) * NZ + shard_z],
            y_ss.at[index, dy], y_rs.at[index, dy], column(dy),
        )

    order = [(r0, 0), (rp1, -1), (rm1, 1), (rp2, -2), (rm2, 2), (rp3, -3), (rm3, 3), (r4, 4)]

    def shard_of(delta):
        return (z + delta + NZ) % NZ

    def serve(index):
        buf, delta = order[index]
        sz = shard_of(delta)

        def one(dy, c):
            w = tab[T_PICK + ((y + dy) % NY) * NZ + sz]
            xs[index * 4 + dy] = buf[:, block_rows(w), :]
            y_copy(dy, index, sz).start()
            return c

        lax.fori_loop(1, NY, one, 0)
        w = tab[T_PICK + y * NZ + sz]
        xr[y * NZ + sz] = buf[:, block_rows(w), :]
        for j in range(2):
            picked = buf[:, block_rows(g_within[j]), :]
            kept = picked.astype(F32) * flag(g_z[j], sz)
            if index == 0:
                gs[j] = kept.astype(BF16)
            else:
                gs[j] = (gs[j].astype(F32) + kept).astype(BF16)

    serve(0)
    for step in (1, 2, 3):
        for half in (0, 1):
            z_copy(step - 1, half, True).wait_recv()
            if step < 3 or half == 0:
                z_copy(step, half, True).start()
            z_copy(step - 1, half, False).wait_recv()
            if step < 3 or half == 1:
                z_copy(step, half, False).start()
        serve(2 * step - 1)
        serve(2 * step)
    z_copy(3, 0, True).wait_recv()
    z_copy(3, 1, False).wait_recv()
    serve(7)

    def gl_copy(dy):
        return remote(gs, gr.at[y], gl_ss.at[dy], gl_rs.at[NY - dy], column(dy))

    def gl_arrival(dy):
        return remote(gs, gr.at[(y + dy) % NY], gl_ss.at[dy], gl_rs.at[dy], column(dy))

    for dy in range(1, NY):
        gl_copy(dy).start()
    gr[y] = gs[...]

    to_after.wait_recv()
    to_before.wait_recv()

    def place(i, s, kb, vb, kt, vt):
        lk[i, s * BS:(s + 1) * BS, :] = kb
        lv[i, s * BS:(s + 1) * BS, :] = vb
        lkt[i, :, s * BS:(s + 1) * BS] = kt
        lvt[i, :, s * BS:(s + 1) * BS] = vt

    def turned(block):
        return block.astype(F32).T.astype(BF16)

    for e in range(QB + 2):
        if e == 0:
            kb, vb = edge[0, 0], edge[0, 1]
        elif e == QB + 1:
            kb, vb = edge[1, 0], edge[1, 1]
        else:
            kb, vb = r0[0, (e - 1) * BS:e * BS, :], r0[1, (e - 1) * BS:e * BS, :]
        kt, vt = turned(kb), turned(vb)
        for s in range(3):
            if 0 <= e - s < QB:
                place(e - s, s, kb, vb, kt, vt)

    for dy in range(1, NY):
        gl_arrival(dy).wait_recv()
    for j in range(2):
        kb, vb = gr[g_y[j], j, 0], gr[g_y[j], j, 1]
        kt, vt = turned(kb), turned(vb)
        for i in range(QB):
            place(i, 3 + j, kb, vb, kt, vt)

    for index in range(8):
        def wait_y(dy, c, index=index):
            y_arrival(dy, index, shard_of(order[index][1])).wait_recv()
            return c
        lax.fori_loop(1, NY, wait_y, 0)

    def place_random(i, c):
        for r in range(RAND):
            owner = tab[T_OWN + i * RAND + r]
            kb, vb = xr[owner, 0], xr[owner, 1]
            place(i, 5 + r, kb, vb, turned(kb), turned(vb))
        return c

    lax.fori_loop(0, QB, place_random, 0)

    own_q.wait()
    own_g.wait()

    def wait_qg(k, c):
        h = (head + k) % NH
        q_arrival(h).wait_recv()
        g_arrival(h).wait_recv()
        return c

    lax.fori_loop(1, NH, wait_qg, 0)

    def attend(j):
        rows = pl.ds(pl.multiple_of(j * CHUNK, CHUNK), CHUNK)
        i = j // 4
        q = qh[rows, :]
        g = gh[rows, :]
        st = dot(lk[i], q, ((1,), (1,)))
        peak = jnp.max(st, axis=0, keepdims=True)
        ex = jnp.exp2((st - peak) * (SCALE * LOG2E))
        inv = 1.0 / jnp.sum(ex, axis=0, keepdims=True)
        pt = ex * inv
        pb = pt.astype(BF16)
        ot = dot(lvt[i], pb, ((1,), (0,)))
        o = ot.T.astype(BF16)
        ob[rows, :] = o
        gt = g.astype(F32).T
        delta = jnp.sum(ot.astype(BF16).astype(F32) * gt, axis=0, keepdims=True)
        dpt = dot(lv[i], g, ((1,), (1,)))
        ds = (pt * (dpt - delta)).astype(BF16)
        dqt = dot(lkt[i], ds, ((1,), (0,))) * SCALE
        dqb[rows, :] = dqt.T.astype(BF16)
        dv = dot(pb, g, ((1,), (0,)))
        dk = dot(ds, q, ((1,), (0,)))
        base = pl.multiple_of(i * BS, BS)
        rbase = pl.multiple_of(i * RAND * BS, BS)
        awk[pl.ds(base, 3 * BS), :] += dk[0:3 * BS]
        awv[pl.ds(base, 3 * BS), :] += dv[0:3 * BS]
        agk[...] += dk[3 * BS:5 * BS]
        agv[...] += dv[3 * BS:5 * BS]
        ark[pl.ds(rbase, RAND * BS), :] += dk[5 * BS:]
        arv[pl.ds(rbase, RAND * BS), :] += dv[5 * BS:]

    def there_rows(h):
        return pl.ds(pl.multiple_of(h * ROWS, 256), ROWS)

    def o_copy(h):
        return remote(ob.at[there_rows(h), :], o_out.at[head], o_ss.at[h], o_rs.at[head], (blk, h))

    def dq_copy(h):
        return remote(dqb.at[there_rows(h), :], dq_out.at[head], dq_ss.at[h], dq_rs.at[head], (blk, h))

    def o_arrival(h):
        return remote(ob.at[there_rows(h), :], o_out.at[h], o_ss.at[h], o_rs.at[h], (blk, h))

    def dq_arrival(h):
        return remote(dqb.at[there_rows(h), :], dq_out.at[h], dq_ss.at[h], dq_rs.at[h], (blk, h))

    own_o = pltpu.make_async_copy(ob.at[there_rows(head), :], o_out.at[head], loc.at[3])
    own_dq = pltpu.make_async_copy(dqb.at[there_rows(head), :], dq_out.at[head], loc.at[4])

    def attend_part(n, c):
        h = (2 * x + 2 + n) % NH

        def chunk(t, cc):
            attend(h * 3 + t)
            return cc

        lax.fori_loop(0, 3, chunk, 0)

        @pl.when(h != head)
        def _():
            o_copy(h).start()
            dq_copy(h).start()

        return c

    lax.fori_loop(0, NH, attend_part, 0)
    own_o.start()
    own_dq.start()

    out_edge = [0, QB + 1]
    for n in range(2):
        rows = slice(out_edge[n] * BS, (out_edge[n] + 1) * BS)
        es[n, 0] = (awk[rows, :] * SCALE).astype(BF16)
        es[n, 1] = awv[rows, :].astype(BF16)
    e2_before = remote(es.at[0], er.at[1], e2_ss.at[0], e2_rs.at[1], before)
    e2_after = remote(es.at[1], er.at[0], e2_ss.at[1], e2_rs.at[0], after)
    e2_before.start()
    e2_after.start()

    gs2[0] = (agk[...] * SCALE).astype(BF16)
    gs2[1] = agv[...].astype(BF16)

    def gl2_copy(dy):
        return remote(gs2, gr2.at[y], gl2_ss.at[dy], gl2_rs.at[NY - dy], column(dy))

    def gl2_arrival(dy):
        return remote(gs2, gr2.at[(y + dy) % NY], gl2_ss.at[dy], gl2_rs.at[dy], column(dy))

    for dy in range(1, NY):
        gl2_copy(dy).start()
    gr2[y] = gs2[...]

    def w_copy(dy, index):
        return remote(
            ys.at[index * 4 + dy], yr.at[index * 4 + y],
            w_ss.at[index, dy], w_rs.at[index, (NY - dy) % NY], column(dy),
        )

    def w_arrival(dy, index):
        return remote(
            ys.at[index * 4 + dy], yr.at[index * 4 + (y + dy) % NY],
            w_ss.at[index, dy], w_rs.at[index, dy], column(dy),
        )

    back = [4, 3, -3, 2, -2, 1, -1, 0]

    def slot_rows(slot):
        return pl.ds(slot * BS, BS)

    for index, delta in enumerate(back):
        sz = shard_of(delta)

        def give(dy, c, index=index, sz=sz):
            slot = tab[T_SLOT + ((y + dy) % NY) * NZ + sz]
            ys[index * 4 + dy, 0] = (ark[slot_rows(slot), :] * SCALE).astype(BF16)
            ys[index * 4 + dy, 1] = arv[slot_rows(slot), :].astype(BF16)
            w_copy(dy, index).start()
            return c

        lax.fori_loop(1, NY, give, 0)
        slot = tab[T_SLOT + y * NZ + sz]
        yr[index * 4 + y, 0] = (ark[slot_rows(slot), :] * SCALE).astype(BF16)
        yr[index * 4 + y, 1] = arv[slot_rows(slot), :].astype(BF16)

    for dy in range(1, NY):
        gl2_arrival(dy).wait_recv()

    def add_up(index):
        sz = shard_of(back[index])

        def wait_w(dy, c):
            w_arrival(dy, index).wait_recv()
            return c

        lax.fori_loop(1, NY, wait_w, 0)

        def one_block(b, c):
            for half in range(2):
                total = jnp.zeros((BS, DH), F32)
                for yy in range(NY):
                    hit = flag(tab[T_WANT + yy * NZ + sz], b)
                    total += yr[index * 4 + yy, half].astype(F32) * hit
                for j in range(2):
                    hit = flag(glob[j], (y * NZ + sz) * QB + b)
                    summed = jnp.zeros((BS, DH), F32)
                    for yy in range(NY):
                        summed += gr2[yy, half, j * BS:(j + 1) * BS, :].astype(F32)
                    total += summed * hit
                part[half, pl.ds(pl.multiple_of(b * BS, BS), BS), :] = total
            return c

        lax.fori_loop(0, QB, one_block, 0)

    def p_copy(step, half, upward):
        if upward:
            return remote(ssp.at[step, half], srp.at[step, half], pp_ss.at[step, half], pp_rs.at[step, half], up)
        return remote(ssm.at[step, half], srm.at[step, half], pm_ss.at[step, half], pm_rs.at[step, half], down)

    add_up(0)
    ssp[0, 0] = part[0].astype(BF16)
    p_copy(0, 0, True).start()
    ssm[0, 1] = part[1].astype(BF16)
    p_copy(0, 1, False).start()
    for step in (1, 2, 3):
        for upward in (True, False):
            add_up(2 * step - 1 if upward else 2 * step)
            first = 0 if upward else 1
            send, recv = (ssp, srp) if upward else (ssm, srm)
            for half in (first, 1 - first):
                if step > 1 or half == first:
                    p_copy(step - 1, half, upward).wait_recv()
                    send[step, half] = (part[half] + recv[step - 1, half].astype(F32)).astype(BF16)
                else:
                    send[step, half] = part[half].astype(BF16)
                p_copy(step, half, upward).start()
    add_up(7)
    e2_before.wait_send()
    e2_after.wait_send()
    remote(es.at[0], er.at[1], e2_ss.at[0], e2_rs.at[1], before).wait_recv()
    remote(es.at[1], er.at[0], e2_ss.at[1], e2_rs.at[0], after).wait_recv()
    for half, window in ((0, awk), (1, awv)):
        factor = SCALE if half == 0 else 1.0
        p_copy(3, half, True).wait_recv()
        p_copy(3, half, False).wait_recv()
        for b in range(QB):
            rows = slice(b * BS, (b + 1) * BS)
            total = window[(b + 1) * BS:(b + 2) * BS, :] * factor + part[half, rows, :]
            total += srp[3, half, rows, :].astype(F32) + srm[3, half, rows, :].astype(F32)
            if b == 0:
                total += er[0, half].astype(F32)
            if b == QB - 1:
                total += er[1, half].astype(F32)
            dkvb[half, rows, :] = total.astype(BF16)

    def part_rows(h):
        return pl.ds(pl.multiple_of(h * PART, 32), PART)

    def dkv_copy(h):
        return remote(dkvb.at[:, part_rows(h), :], dkv_out.at[head], dkv_ss.at[h], dkv_rs.at[head], (blk, h))

    def dkv_arrival(h):
        return remote(dkvb.at[:, part_rows(h), :], dkv_out.at[h], dkv_ss.at[h], dkv_rs.at[h], (blk, h))

    own_dkv = pltpu.make_async_copy(dkvb.at[:, mine, :], dkv_out.at[head], loc.at[5])

    def send_dkv(k, c):
        dkv_copy((head + k) % NH).start()
        return c

    lax.fori_loop(1, NH, send_dkv, 0)
    own_dkv.start()

    def drain(k, c):
        h = (head + k) % NH
        kv_copy(h).wait_send()
        q_copy(h).wait_send()
        g_copy(h).wait_send()
        o_copy(h).wait_send()
        dq_copy(h).wait_send()
        dkv_copy(h).wait_send()
        o_arrival(h).wait_recv()
        dq_arrival(h).wait_recv()
        dkv_arrival(h).wait_recv()
        return c

    for step in range(4):
        for half in range(2):
            if step < 3 or half == 0:
                z_copy(step, half, True).wait_send()
            if step < 3 or half == 1:
                z_copy(step, half, False).wait_send()
            if step > 0 or half == 0:
                p_copy(step, half, True).wait_send()
            if step > 0 or half == 1:
                p_copy(step, half, False).wait_send()
    to_after.wait_send()
    to_before.wait_send()

    def drain_column(dy, c):
        gl_copy(dy).wait_send()
        gl2_copy(dy).wait_send()
        for index in range(8):
            y_copy(dy, index, shard_of(order[index][1])).wait_send()
            w_copy(dy, index).wait_send()
        return c

    lax.fori_loop(1, NY, drain_column, 0)
    lax.fori_loop(1, NH, drain, 0)
    own_o.wait()
    own_dq.wait()
    own_dkv.wait()


def tables(rand_blocks, global_blocks):
    blk = lax.axis_index("blk")
    head = lax.axis_index("head")
    y, z = blk // NZ, blk % NZ
    chosen = lax.dynamic_slice_in_dim(rand_blocks, head, 1, 1).reshape(NY, NZ, SLOTS)
    column = lax.dynamic_slice_in_dim(chosen, z, 1, 1)
    owners = y * NZ + jnp.arange(NZ, dtype=jnp.int32)[None, :, None]
    want = jnp.max(jnp.where(column // QB == owners, column % QB, -1), axis=2)
    own = lax.dynamic_slice_in_dim(chosen.reshape(NY * NZ, SLOTS), blk, 1, 0)[0] // QB
    shards = jnp.arange(NY * NZ, dtype=jnp.int32)[:, None]
    slot = jnp.max(
        jnp.where(own[None, :] == shards, jnp.arange(SLOTS, dtype=jnp.int32)[None, :], 0), axis=1
    )
    want = want.reshape(-1)
    picked = jnp.maximum(want, 0)
    shard = global_blocks // QB
    return jnp.concatenate(
        [want, picked, own, slot, global_blocks, global_blocks % QB, shard % NZ, shard // NZ]
    )


def on_device(queries, keys, values, out_grad, rand_blocks, global_blocks):
    tab = tables(rand_blocks, global_blocks)
    heads = queries.shape[1] // NH
    q_s = queries.reshape(PART, NH, heads, DH).transpose(1, 0, 2, 3).reshape(NH, ROWS, DH)
    g_s = out_grad.reshape(PART, NH, heads, DH).transpose(1, 0, 2, 3).reshape(NH, ROWS, DH)
    kv_s = jnp.stack([keys, values]).transpose(2, 0, 1, 3)
    vm = lambda shape, dtype=BF16: pltpu.VMEM(shape, dtype)
    dma = lambda *shape: pltpu.SemaphoreType.DMA(shape)
    total = NH * ROWS
    pair = (2, BS, DH)
    anywhere = pl.BlockSpec(memory_space=pl.ANY)
    o_h, dq_h, dkv_h = pl.pallas_call(
        body,
        out_shape=(
            jax.ShapeDtypeStruct((NH, ROWS, DH), BF16),
            jax.ShapeDtypeStruct((NH, ROWS, DH), BF16),
            jax.ShapeDtypeStruct((NH, 2, PART, DH), BF16),
        ),
        in_specs=[pl.BlockSpec(memory_space=pltpu.SMEM), anywhere, anywhere, anywhere],
        out_specs=(anywhere, anywhere, anywhere),
        scratch_shapes=[
            vm((total, DH)), vm((total, DH)),
            *[vm((2, ROWS, DH)) for _ in range(8)],
            vm((32,) + pair), vm((32,) + pair), vm((2,) + pair), vm((2,) + pair), vm((NY, 2) + pair),
            vm((QB, LIST, DH)), vm((QB, LIST, DH)), vm((QB, DH, LIST)), vm((QB, DH, LIST)),
            vm((total, DH)), vm((total, DH)),
            vm(((QB + 2) * BS, DH), F32), vm(((QB + 2) * BS, DH), F32),
            vm((2 * BS, DH), F32), vm((2 * BS, DH), F32),
            vm((SLOTS * BS, DH), F32), vm((SLOTS * BS, DH), F32),
            vm((32,) + pair), vm((32,) + pair), vm((2,) + pair), vm((2,) + pair),
            vm((2, 2 * BS, DH)), vm((NY, 2, 2 * BS, DH)),
            vm((2, ROWS, DH), F32),
            *[vm((4, 2, ROWS, DH)) for _ in range(4)],
            vm((2, ROWS, DH)),
            dma(NH), dma(NH), dma(NH), dma(NH), dma(NH), dma(NH), dma(6),
            dma(4, 2), dma(4, 2), dma(4, 2), dma(4, 2), dma(2), dma(2), dma(8, NY), dma(8, NY),
            dma(NY), dma(NY),
            dma(NH), dma(NH), dma(NH), dma(NH), dma(8, NY), dma(8, NY), dma(2), dma(2),
            dma(NY), dma(NY),
            dma(4, 2), dma(4, 2), dma(4, 2), dma(4, 2), dma(NH), dma(NH),
        ],
        compiler_params=pltpu.CompilerParams(
            collective_id=0, has_side_effects=True, vmem_limit_bytes=60 * 2**20
        ),
    )(tab, q_s, g_s, kv_s)

    def rows_back(part):
        return part.reshape(NH, PART, heads, DH).transpose(1, 0, 2, 3).reshape(PART, NH * heads, DH)

    kv_back = dkv_h.transpose(1, 2, 0, 3)
    return rows_back(o_h), rows_back(dq_h), kv_back[0], kv_back[1]


def solution(mesh):
    rows = P(("blk", "head"), None, None)
    return jax.shard_map(
        on_device,
        mesh=mesh,
        in_specs=(rows, rows, rows, rows, P(), P()),
        out_specs=(rows, rows, rows, rows),
        check_vma=False,
    )
```

time: 613 us -> 176 us (0.29)
  waiting for transfers between devices: 314 us -> 0 us
  Pallas kernels: 0 us -> 161 us
  matrix products: 97 us -> 0 us
  local copies, waits for them, and re-layouts: 91.3 us -> 12.1 us
  starting transfers between devices: 46.3 us -> 0 us
  blocking collectives: 22.1 us -> 0 us
  other arithmetic: 21.2 us -> 1.98 us
  between operations: 14.8 us -> 0.77 us
    all_to_all x8 -> x0, waiting for transfers between devices: 209 us -> none  [the longest x1 85.4 us: on_device(): lax.all_to_all(pack_k, 'blk', split_axis=0, concat_axis=0, tiled=True)]
    pallas_call x0 -> x1, Pallas kernels: none -> 161 us  [on_device(): pl.pallas_call(body, out_shape=(jax.ShapeDtypeStruct((NH, ROWS, DH), BF16...]
    all_gather x2 -> x0, waiting for transfers between devices: 105 us -> none  [the longest x1 81.4 us: on_device(): lax.all_gather(cycle_keys, 'blk', axis=0, tiled=True)]
    dot_general x42 -> x0, matrix products: 97 us -> none  [the longest x6 21.1 us: attend_rows(): jnp.einsum('tgad,gkd->gatk', grad_blk, value_blk, preferred_element_type=...]
    all_to_all x8 -> x0, starting transfers between devices: 46.2 us -> none  [the longest x1 8.69 us: on_device(): lax.all_to_all(dv_rows, 'head', split_axis=0, concat_axis=1, tiled=True)]
    all_to_all x2 -> x0, blocking collectives: 22.1 us -> none  [the longest x1 12.2 us: on_device(): lax.all_to_all(values, 'head', split_axis=1, concat_axis=0, tiled=True)]
    scatter-add x6 -> x0, local copies, waits for them, and re-layouts: 18.2 us -> none  [spread(): extended.at[:, offset:offset + blocks_here].add(moved[:, :, offset])]
    unnamed x32 -> x10, local copies, waits for them, and re-layouts: 17.1 us -> 1.53 us
  transfers between devices with their start and end apart: 10 -> 0, of which waited for: 8 -> 0; matrix products, arithmetic and copies ran while one was open for 15% -> 0% of each run, Pallas kernels for 0% -> 0%
where the time goes in v1:
time: 176 us
  Pallas kernels  161 us (91%)
  local copies, waits for them, and re-layouts  12.1 us (7%)
  other arithmetic  1.98 us (1%)
    pallas_call x1, Pallas kernels, on_device(): pl.pallas_call(body, out_shape=(jax.ShapeDtypeStruct((NH, ROWS, DH), BF16...  161 us
    reshape x2, local copies, waits for them, and re-layouts, rows_back(): part.reshape(NH, PART, heads, DH).transpose(1, 0, 2, 3)  4.64 us

profile of v1, /device:TPU:1, one launch (start us, length us, event | category | flops | bytes accessed | tf_op | source)
XLA Modules:
  0.0 176.2 jit_solution(10207355458890839265)
XLA Ops:
  0.6 0.0 copy-start
  0.6 0.0 copy-start.2
  0.7 0.8 and_select_fusion.2
  1.5 0.8 constant_dynamic-slice_fusion.1
  2.3 0.1 copy.28
  2.5 0.1 reshape_reshape.3
  2.6 0.1 reshape.53
  2.7 0.2 select_reduce_fusion
  2.9 0.1 reshape.54
  3.0 0.1 select_reduce_fusion.1
  3.1 1.3 concatenate.3.tab
  4.4 1.1 copy_bitcast_fusion.4
  5.5 0.8 maximum_bitcast_fusion.kv_s
  6.2 0.0 copy-done
  6.3 0.0 copy-done.2
  6.3 2.4 %copy_bitcast_fusion.2 = (bf16[8,768,128]{2,1,0:T(8,128)(2,1)}, bf16[8,768,128]{2,1,0:T(8,128)(2,1)}) fusion(bf16[96,64,128]{2,1,0:T(8,128)(2,1)S(1)} %copy-done, bf16[96,64,128]{2,1,0:T(8,128)(2,1)S(1)} %copy-done.2), kind=kLoop, calls=%fused_computation.2 | loop fusion | bytes 6291456 | tf_op jit(solution)/shard_map/reshape | solution.py:563
  8.7 161.3 %shard_map.93 = (bf16[8,768,128]{2,1,0:T(8,128)(2,1)}, bf16[8,768,128]{2,1,0:T(8,128)(2,1)}, bf16[8,2,96,128]{3,2,1,0:T(8,128)(2,1)}) custom-call(s32[122]{0:T(128)} %concatenate.3.tab, bf16[8,768,128]{2,1,0:T(8,128)(2,1)} %get-tuple-element.35.q_s, bf16[8,768,128]{2,1,0:T(8,128)(2,1)} %get-tuple-element.34.g_s, bf16[8,2,96,128]{3,2,1,0:T(8,128)(2,1)} %maximum_bitcast_fusion.kv_s), custom_call_target="tpu_custom_call" | custom-call | tf_op jit(solution)/shard_map/pallas_call | solution.py:570
  170.0 0.0 copy-start.3
  170.0 3.0 %copy_bitcast_fusion.1 = bf16[96,64,128]{2,1,0:T(8,128)(2,1)} fusion(bf16[8,768,128]{2,1,0:T(8,128)(2,1)} %get-tuple-element.7), kind=kLoop, calls=%fused_computation.1 | loop fusion | bytes 3145728 | tf_op jit(solution)/shard_map/reshape | solution.py:606
  173.1 0.0 copy-done.3
  173.1 0.0 copy-start.1
  173.1 0.8 copy.37
  173.9 0.8 copy.36
  174.6 0.0 copy-done.1
  174.6 1.6 copy_bitcast_fusion
  (7 shorter events, 0.1 us)
Async XLA Ops:
  0.6 5.6 %copy-start = (bf16[96,64,128]{2,1,0:T(8,128)(2,1)S(1)}, bf16[96,64,128]{2,1,0:T(8,128)(2,1)}, u32[]{:S(2)}) copy-start(bf16[96,64,128]{2,1,0:T(8,128)(2,1)} %param.6) | copy-start | bytes 4718596
  0.6 5.6 %copy-start.2 = (bf16[96,64,128]{2,1,0:T(8,128)(2,1)S(1)}, bf16[96,64,128]{2,1,0:T(8,128)(2,1)}, u32[]{:S(2)}) copy-start(bf16[96,64,128]{2,1,0:T(8,128)(2,1)} %param.9) | copy-start | bytes 4718596
  170.0 3.1 %copy-start.3 = (bf16[8,2,96,128]{3,2,1,0:T(8,128)(2,1)S(1)}, bf16[8,2,96,128]{3,2,1,0:T(8,128)(2,1)}, u32[]{:S(2)}) copy-start(bf16[8,2,96,128]{3,2,1,0:T(8,128)(2,1)} %get-tuple-element.9) | copy-start | bytes 1179652
  173.1 1.5 copy-start.1

commit v2 on v1

v2 whole, which is shorter than its diff:
```python
import functools
import math

import jax
import jax.numpy as jnp
from jax import lax
from jax.experimental import pallas as pl
from jax.experimental.pallas import tpu as pltpu
from jax.sharding import PartitionSpec as P

MESH = pl.DeviceIdType.MESH
NY, NZ, NH = 4, 8, 8
QB, BS, DH, RAND = 6, 128, 128, 3
ROWS = QB * BS
PART = ROWS // NH
LIST = 8 * BS
CHUNK = 256
NEAR, FAR = 5 * BS, RAND * BS
CHUNKS = NH * ROWS // CHUNK
PIECE = BS // NZ
SLOTS = QB * RAND
SCALE = 1.0 / math.sqrt(DH)
LOG2E = 1.4426950408889634
F32, BF16 = jnp.float32, jnp.bfloat16

T_WANT, T_PICK, T_OWN, T_SLOT, T_GLOB = 0, 32, 64, 82, 114


def dot(a, b, dims):
    return lax.dot_general(a, b, (dims, ((), ())), preferred_element_type=F32)


def flag(a, b):
    return (a == b).astype(jnp.int32).astype(F32)


def body(
    tab, q_s, g_s, kv_s, o_out, dq_out, dkv_out,
    qh, gh, r0, rp1, rp2, rp3, rm1, rm2, rm3, r4, xs, xr, edge,
    lkn, lvn, lktn, lvtn, lkf, lvf, lktf, lvtf, exn, dsf, o1, stats, ob, dqb,
    awk, awv, agk, agv, ark, arv,
    ys, yr, es, er, partp, partm, ssp, ssm, srp, srm, dkvb,
    ga, gy, gp, gz, gm, gf, gall,
    head_ss, head_rs, q_ss, q_rs, g_ss, g_rs, loc,
    zp_ss, zp_rs, zm_ss, zm_rs, e_ss, e_rs, y_ss, y_rs,
    a0_ss, a0_rs, a1_ss, a1_rs, a2_ss, a2_rs, a3_ss, a3_rs,
    o_ss, o_rs, dq_ss, dq_rs, w_ss, w_rs, e2_ss, e2_rs,
    pp_ss, pp_rs, pm_ss, pm_rs, dkv_ss, dkv_rs,
):
    blk = lax.axis_index("blk")
    head = lax.axis_index("head")
    y, z = blk // NZ, blk % NZ
    x, core = head // 2, head % 2
    up = (y * NZ + (z + 1) % NZ, head)
    down = (y * NZ + (z + NZ - 1) % NZ, head)
    after = ((blk + 1) % (NY * NZ), head)
    before = ((blk + NY * NZ - 1) % (NY * NZ), head)

    def column(dy):
        return (((y + dy) % NY) * NZ + z, head)

    def ring(dz):
        return (y * NZ + (z + dz) % NZ, head)

    def peer(k):
        t = k // 2
        return ((x + t * (t + 1) // 2) % (NH // 2)) * 2 + (core + k) % 2

    def remote(src, dst, ss, rs, dev):
        return pltpu.make_async_remote_copy(
            src_ref=src, dst_ref=dst, send_sem=ss, recv_sem=rs, device_id=dev, device_id_type=MESH
        )

    bar = pltpu.get_barrier_semaphore()

    def greet(dev):
        pl.semaphore_signal(bar, inc=1, device_id=dev, device_id_type=MESH)

    def greet_head(k, c):
        greet((blk, (head + k) % NH))
        return c

    lax.fori_loop(1, NH, greet_head, 0)
    for dev in (after, before):
        greet(dev)
    for dy in range(1, NY):
        greet(column(dy))

    def greet_ring(dz, c):
        greet(ring(dz))
        return c

    lax.fori_loop(1, NZ, greet_ring, 0)
    pl.semaphore_wait(bar, NH - 1 + 2 + NY - 1 + NZ - 1)

    mine = pl.ds(pl.multiple_of(head * PART, 32), PART)
    rows_mine = pl.ds(pl.multiple_of(head * ROWS, 256), ROWS)

    def kv_copy(h):
        return remote(kv_s.at[h], r0.at[:, mine, :], head_ss.at[h], head_rs.at[head], (blk, h))

    def kv_arrival(h):
        there = pl.ds(pl.multiple_of(h * PART, 32), PART)
        return remote(kv_s.at[h], r0.at[:, there, :], head_ss.at[h], head_rs.at[h], (blk, h))

    def q_copy(h):
        return remote(q_s.at[h], qh.at[rows_mine, :], q_ss.at[h], q_rs.at[head], (blk, h))

    def g_copy(h):
        return remote(g_s.at[h], gh.at[rows_mine, :], g_ss.at[h], g_rs.at[head], (blk, h))

    def q_arrival(h):
        there = pl.ds(pl.multiple_of(h * ROWS, 256), ROWS)
        return remote(q_s.at[h], qh.at[there, :], q_ss.at[h], q_rs.at[h], (blk, h))

    def g_arrival(h):
        there = pl.ds(pl.multiple_of(h * ROWS, 256), ROWS)
        return remote(g_s.at[h], gh.at[there, :], g_ss.at[h], g_rs.at[h], (blk, h))

    own_kv = pltpu.make_async_copy(kv_s.at[head], r0.at[:, mine, :], loc.at[0])
    own_q = pltpu.make_async_copy(q_s.at[head], qh.at[rows_mine, :], loc.at[1])
    own_g = pltpu.make_async_copy(g_s.at[head], gh.at[rows_mine, :], loc.at[2])
    own_kv.start()

    def send_kv(k, c):
        kv_copy(peer(k)).start()
        return c

    def send_q(k, c):
        q_copy(peer(k)).start()
        return c

    def send_g(k, c):
        g_copy(peer(k)).start()
        return c

    lax.fori_loop(1, NH, send_kv, 0)
    own_q.start()
    own_g.start()
    lax.fori_loop(1, NH, send_q, 0)
    lax.fori_loop(1, NH, send_g, 0)

    zero = jnp.zeros((BS, DH), F32)
    for ref in (awk, awv, agk, agv, ark, arv):
        def clear(n, c, ref=ref):
            ref[pl.ds(pl.multiple_of(n * BS, BS), BS), :] = zero
            return c
        lax.fori_loop(0, ref.shape[0] // BS, clear, 0)

    own_kv.wait()

    def wait_kv(k, c):
        kv_arrival((head + k) % NH).wait_recv()
        return c

    lax.fori_loop(1, NH, wait_kv, 0)

    plus = [r0, rp1, rp2, rp3, r4]
    minus = [r0, rm1, rm2, rm3, r4]

    def z_copy(step, half, upward):
        chain = plus if upward else minus
        ss, rs = (zp_ss, zp_rs) if upward else (zm_ss, zm_rs)
        return remote(
            chain[step].at[half], chain[step + 1].at[half],
            ss.at[step, half], rs.at[step, half], up if upward else down,
        )

    to_after = remote(r0.at[:, pl.ds(ROWS - BS, BS), :], edge.at[0], e_ss.at[0], e_rs.at[0], after)
    to_before = remote(r0.at[:, pl.ds(0, BS), :], edge.at[1], e_ss.at[1], e_rs.at[1], before)
    for half in (0, 1):
        z_copy(0, half, True).start()
        z_copy(0, half, False).start()
    to_after.start()
    to_before.start()

    glob = [tab[T_GLOB + j] for j in range(2)]
    g_within = [tab[T_GLOB + 2 + j] for j in range(2)]

    def ar_y(n, dy):
        return remote(ga.at[n, (y + dy) % NY], gy.at[n, y], a0_ss.at[n, dy], a0_rs.at[n, NY - dy], column(dy))

    def ar_z(n, dz):
        rows = pl.ds(pl.multiple_of(((z + dz) % NZ) * PIECE, PIECE), PIECE)
        return remote(gp.at[n, rows, :], gz.at[n, z], a1_ss.at[n, dz], a1_rs.at[n, NZ - dz], ring(dz))

    z_rows = pl.ds(pl.multiple_of(z * PIECE, PIECE), PIECE)

    def ar_zback(n, dz):
        return remote(gm.at[n], gf.at[n, z_rows, :], a2_ss.at[n, dz], a2_rs.at[n, NZ - dz], ring(dz))

    def ar_yback(n, dy):
        return remote(gf.at[n], gall.at[n, y], a3_ss.at[n, dy], a3_rs.at[n, NY - dy], column(dy))

    def each(count, make, what):
        def one(d, c):
            copy = make(d)
            copy.start() if what == "start" else copy.wait_send()
            return c
        lax.fori_loop(1, count, one, 0)

    def ar_start(n):
        each(NY, functools.partial(ar_y, n), "start")
        gy[n, y] = ga[n, y]

    def ar_one(n):
        for dy in range(1, NY):
            remote(ga.at[n, y], gy.at[n, (y + dy) % NY], a0_ss.at[n, dy], a0_rs.at[n, dy], column(dy)).wait_recv()
        total = gy[n, 0].astype(F32)
        for k in range(1, NY):
            total += gy[n, k].astype(F32)
        gp[n] = total.astype(BF16)
        each(NZ, functools.partial(ar_z, n), "start")
        gz[n, z] = gp[n, z_rows, :]

    def ar_two(n):
        for dz in range(1, NZ):
            remote(gm.at[n], gz.at[n, (z + dz) % NZ], a1_ss.at[n, dz], a1_rs.at[n, dz], ring(dz)).wait_recv()
        total = gz[n, 0].astype(F32)
        for k in range(1, NZ):
            total += gz[n, k].astype(F32)
        gm[n] = total.astype(BF16)
        each(NZ, functools.partial(ar_zback, n), "start")
        gf[n, z_rows, :] = gm[n]

    def ar_three(n):
        for dz in range(1, NZ):
            rows = pl.ds(pl.multiple_of(((z + dz) % NZ) * PIECE, PIECE), PIECE)
            remote(gm.at[n], gf.at[n, rows, :], a2_ss.at[n, dz], a2_rs.at[n, dz], ring(dz)).wait_recv()
        each(NY, functools.partial(ar_yback, n), "start")
        gall[n, y] = gf[n]

    def ar_end(n):
        for dy in range(1, NY):
            remote(gf.at[n], gall.at[n, (y + dy) % NY], a3_ss.at[n, dy], a3_rs.at[n, dy], column(dy)).wait_recv()

    def ar_drain(n):
        each(NY, functools.partial(ar_y, n), "wait")
        each(NZ, functools.partial(ar_z, n), "wait")
        each(NZ, functools.partial(ar_zback, n), "wait")
        each(NY, functools.partial(ar_yback, n), "wait")

    def block_rows(w):
        return pl.ds(w * BS, BS)

    def y_copy(dy, index, shard_z):
        dev = column(dy)
        return remote(
            xs.at[index * 4 + dy], xr.at[y * NZ + shard_z],
            y_ss.at[index, dy], y_rs.at[index, (NY - dy) % NY], dev,
        )

    def y_arrival(dy, index, shard_z):
        return remote(
            xs.at[index * 4 + dy], xr.at[((y + dy) % NY) * NZ + shard_z],
            y_ss.at[index, dy], y_rs.at[index, dy], column(dy),
        )

    order = [(r0, 0), (rp1, -1), (rm1, 1), (rp2, -2), (rm2, 2), (rp3, -3), (rm3, 3), (r4, 4)]

    def shard_of(delta):
        return (z + delta + NZ) % NZ

    def serve(index):
        buf, delta = order[index]
        sz = shard_of(delta)

        def one(dy, c):
            w = tab[T_PICK + ((y + dy) % NY) * NZ + sz]
            xs[index * 4 + dy] = buf[:, block_rows(w), :]
            y_copy(dy, index, sz).start()
            return c

        lax.fori_loop(1, NY, one, 0)
        w = tab[T_PICK + y * NZ + sz]
        xr[y * NZ + sz] = buf[:, block_rows(w), :]
    def place(i, s, kb, vb):
        if s < 5:
            k_list, v_list, kt_list, vt_list, at = lkn, lvn, lktn, lvtn, s * BS
        else:
            k_list, v_list, kt_list, vt_list, at = lkf, lvf, lktf, lvtf, (s - 5) * BS
        k_list[i, at:at + BS, :] = kb
        v_list[i, at:at + BS, :] = vb
        kt_list[i, :, at:at + BS] = turned(kb)
        vt_list[i, :, at:at + BS] = turned(vb)

    def turned(block):
        return block.astype(F32).T.astype(BF16)

    def place_window(e, kb, vb):
        for s in range(3):
            if 0 <= e - s < QB:
                place(e - s, s, kb, vb)

    def attend_near(j):
        rows = pl.ds(pl.multiple_of(j * CHUNK, CHUNK), CHUNK)
        i = j // 4
        q = qh[rows, :]
        st = dot(lkn[i], q, ((1,), (1,)))
        peak = jnp.max(st, axis=0, keepdims=True)
        ex = jnp.exp2((st - peak) * (SCALE * LOG2E))
        stats[j, 0:1, :] = peak
        stats[j, 1:2, :] = jnp.sum(ex, axis=0, keepdims=True)
        eb = ex.astype(BF16)
        exn[j] = eb
        o1[j] = dot(lvtn[i], eb, ((1,), (0,)))

    def attend_far(j):
        rows = pl.ds(pl.multiple_of(j * CHUNK, CHUNK), CHUNK)
        i = j // 4
        q = qh[rows, :]
        g = gh[rows, :]
        st = dot(lkf[i], q, ((1,), (1,)))
        dpt = dot(lvf[i], g, ((1,), (1,)))
        gt = g.astype(F32).T
        before_peak = stats[j, 0:1, :]
        peak = jnp.maximum(before_peak, jnp.max(st, axis=0, keepdims=True))
        shrink = jnp.exp2((before_peak - peak) * (SCALE * LOG2E))
        ex = jnp.exp2((st - peak) * (SCALE * LOG2E))
        inv = 1.0 / (shrink * stats[j, 1:2, :] + jnp.sum(ex, axis=0, keepdims=True))
        near = shrink * inv
        pt = ex * inv
        pb = pt.astype(BF16)
        ot = o1[j] * near + dot(lvtf[i], pb, ((1,), (0,)))
        ob[rows, :] = ot.T.astype(BF16)
        delta = jnp.sum(ot.astype(BF16).astype(F32) * gt, axis=0, keepdims=True)
        stats[j, 2:3, :] = near
        stats[j, 3:4, :] = delta
        ds = (pt * (dpt - delta)).astype(BF16)
        dsf[j] = ds
        rbase = pl.multiple_of(i * FAR, BS)
        arv[pl.ds(rbase, FAR), :] += dot(pb, g, ((1,), (0,)))
        ark[pl.ds(rbase, FAR), :] += dot(ds, q, ((1,), (0,)))

    def attend_back(j):
        rows = pl.ds(pl.multiple_of(j * CHUNK, CHUNK), CHUNK)
        i = j // 4
        q = qh[rows, :]
        g = gh[rows, :]
        dpt = dot(lvn[i], g, ((1,), (1,)))
        pt = exn[j].astype(F32) * stats[j, 2:3, :]
        pb = pt.astype(BF16)
        ds = (pt * (dpt - stats[j, 3:4, :])).astype(BF16)
        dqt = dot(lktn[i], ds, ((1,), (0,))) + dot(lktf[i], dsf[j], ((1,), (0,)))
        dqb[rows, :] = (dqt * SCALE).T.astype(BF16)
        dv = dot(pb, g, ((1,), (0,)))
        dk = dot(ds, q, ((1,), (0,)))
        base = pl.multiple_of(i * BS, BS)
        awk[pl.ds(base, 3 * BS), :] += dk[0:3 * BS]
        awv[pl.ds(base, 3 * BS), :] += dv[0:3 * BS]
        agk[...] += dk[3 * BS:]
        agv[...] += dv[3 * BS:]

    def three(h, what):
        def chunk(t, c):
            what(h * 3 + t)
            return c
        lax.fori_loop(0, 3, chunk, 0)

    def near_parts(first, last):
        def part(k, c):
            h = peer(k)

            @pl.when(k > 0)
            def _():
                q_arrival(h).wait_recv()

            three(h, attend_near)
            return c

        lax.fori_loop(first, last, part, 0)

    for j in range(2):
        here = flag(tab[T_GLOB + 4 + j], blk)
        for half in range(2):
            picked = r0[half, block_rows(g_within[j]), :].astype(F32)
            ga[0, 2 * j + half] = (picked * here).astype(BF16)
    ar_start(0)
    serve(0)
    for e in range(1, QB + 1):
        place_window(e, r0[0, (e - 1) * BS:e * BS, :], r0[1, (e - 1) * BS:e * BS, :])
    ar_one(0)

    def forward(step, half):
        z_copy(step - 1, half, True).wait_recv()
        if step < 3 or half == 0:
            z_copy(step, half, True).start()
        z_copy(step - 1, half, False).wait_recv()
        if step < 3 or half == 1:
            z_copy(step, half, False).start()

    forward(1, 0)
    ar_two(0)
    to_after.wait_recv()
    to_before.wait_recv()
    place_window(0, edge[0, 0], edge[0, 1])
    place_window(QB + 1, edge[1, 0], edge[1, 1])
    forward(1, 1)
    serve(1)
    serve(2)
    ar_three(0)
    forward(2, 0)
    ar_end(0)
    for j in range(2):
        for i in range(QB):
            place(i, 3 + j, gall[0, 2 * j], gall[0, 2 * j + 1])
    forward(2, 1)
    serve(3)
    serve(4)
    own_q.wait()
    near_parts(0, 2)
    forward(3, 0)
    near_parts(2, 4)
    forward(3, 1)
    serve(5)
    serve(6)
    near_parts(4, 6)
    z_copy(3, 0, True).wait_recv()
    z_copy(3, 1, False).wait_recv()
    serve(7)
    near_parts(6, 8)

    for index in range(8):
        def wait_y(dy, c, index=index):
            y_arrival(dy, index, shard_of(order[index][1])).wait_recv()
            return c
        lax.fori_loop(1, NY, wait_y, 0)

    def place_random(i, c):
        for r in range(RAND):
            owner = tab[T_OWN + i * RAND + r]
            place(i, 5 + r, xr[owner, 0], xr[owner, 1])
        return c

    lax.fori_loop(0, QB, place_random, 0)
    own_g.wait()

    def wait_g(k, c):
        g_arrival(peer(k)).wait_recv()
        return c

    lax.fori_loop(1, NH, wait_g, 0)

    def there_rows(h):
        return pl.ds(pl.multiple_of(h * ROWS, 256), ROWS)

    def o_copy(h):
        return remote(ob.at[there_rows(h), :], o_out.at[head], o_ss.at[h], o_rs.at[head], (blk, h))

    def dq_copy(h):
        return remote(dqb.at[there_rows(h), :], dq_out.at[head], dq_ss.at[h], dq_rs.at[head], (blk, h))

    def o_arrival(h):
        return remote(ob.at[there_rows(h), :], o_out.at[h], o_ss.at[h], o_rs.at[h], (blk, h))

    def dq_arrival(h):
        return remote(dqb.at[there_rows(h), :], dq_out.at[h], dq_ss.at[h], dq_rs.at[h], (blk, h))

    own_o = pltpu.make_async_copy(ob.at[there_rows(head), :], o_out.at[head], loc.at[3])
    own_dq = pltpu.make_async_copy(dqb.at[there_rows(head), :], dq_out.at[head], loc.at[4])

    def far_part(n, c):
        k = NH - 1 - n
        h = peer(k)
        three(h, attend_far)

        @pl.when(k > 0)
        def _():
            o_copy(h).start()

        return c

    lax.fori_loop(0, NH, far_part, 0)
    own_o.start()

    def back_parts(first, last):
        def part(n, c):
            k = NH - 1 - n
            h = peer(k)
            three(h, attend_back)

            @pl.when(k > 0)
            def _():
                dq_copy(h).start()

            return c

        lax.fori_loop(first, last, part, 0)

    def w_copy(dy, index):
        return remote(
            ys.at[index * 4 + dy], yr.at[index * 4 + y],
            w_ss.at[index, dy], w_rs.at[index, (NY - dy) % NY], column(dy),
        )

    def w_arrival(dy, index):
        return remote(
            ys.at[index * 4 + dy], yr.at[index * 4 + (y + dy) % NY],
            w_ss.at[index, dy], w_rs.at[index, dy], column(dy),
        )

    back = [4, 3, -3, 2, -2, 1, -1, 0]

    def slot_rows(slot):
        return pl.ds(slot * BS, BS)

    for index, delta in enumerate(back):
        sz = shard_of(delta)

        def give(dy, c, index=index, sz=sz):
            slot = tab[T_SLOT + ((y + dy) % NY) * NZ + sz]
            ys[index * 4 + dy, 0] = (ark[slot_rows(slot), :] * SCALE).astype(BF16)
            ys[index * 4 + dy, 1] = arv[slot_rows(slot), :].astype(BF16)
            w_copy(dy, index).start()
            return c

        lax.fori_loop(1, NY, give, 0)
        slot = tab[T_SLOT + y * NZ + sz]
        yr[index * 4 + y, 0] = (ark[slot_rows(slot), :] * SCALE).astype(BF16)
        yr[index * 4 + y, 1] = arv[slot_rows(slot), :].astype(BF16)

    def add_up(index, part):
        sz = shard_of(back[index])

        def wait_w(dy, c):
            w_arrival(dy, index).wait_recv()
            return c

        lax.fori_loop(1, NY, wait_w, 0)
        hits = [tab[T_WANT + yy * NZ + sz] for yy in range(NY)]

        def one_block(b, c):
            for half in range(2):
                total = yr[index * 4, half].astype(F32) * flag(hits[0], b)
                for yy in range(1, NY):
                    total += yr[index * 4 + yy, half].astype(F32) * flag(hits[yy], b)
                part[half, pl.ds(pl.multiple_of(b * BS, BS), BS), :] = total
            return c

        lax.fori_loop(0, QB, one_block, 0)

    def p_copy(step, half, upward):
        if upward:
            return remote(ssp.at[step, half], srp.at[step, half], pp_ss.at[step, half], pp_rs.at[step, half], up)
        return remote(ssm.at[step, half], srm.at[step, half], pm_ss.at[step, half], pm_rs.at[step, half], down)

    def pass_on(step):
        for waits in (False, True):
            for upward in (True, False):
                send, recv, part = (ssp, srp, partp) if upward else (ssm, srm, partm)
                first = 0 if upward else 1
                for half in (first, 1 - first):
                    if waits != (step > 1 or half == first):
                        continue
                    total = part[half]
                    if waits:
                        p_copy(step - 1, half, upward).wait_recv()
                        total += recv[step - 1, half].astype(F32)
                    send[step, half] = total.astype(BF16)
                    p_copy(step, half, upward).start()

    back_parts(0, 2)
    add_up(0, partp)
    ssp[0, 0] = partp[0].astype(BF16)
    p_copy(0, 0, True).start()
    ssm[0, 1] = partp[1].astype(BF16)
    p_copy(0, 1, False).start()
    back_parts(2, 4)
    add_up(1, partp)
    add_up(2, partm)
    pass_on(1)
    add_up(3, partp)
    add_up(4, partm)
    back_parts(4, 7)
    pass_on(2)
    add_up(5, partp)
    add_up(6, partm)
    back_parts(7, 8)
    own_dq.start()
    for n, at in ((0, 0), (1, QB + 1)):
        rows = slice(at * BS, (at + 1) * BS)
        es[n, 0] = (awk[rows, :] * SCALE).astype(BF16)
        es[n, 1] = awv[rows, :].astype(BF16)
    e2_before = remote(es.at[0], er.at[1], e2_ss.at[0], e2_rs.at[1], before)
    e2_after = remote(es.at[1], er.at[0], e2_ss.at[1], e2_rs.at[0], after)
    e2_before.start()
    e2_after.start()
    for j in range(2):
        rows = slice(j * BS, (j + 1) * BS)
        ga[1, 2 * j] = (agk[rows, :] * SCALE).astype(BF16)
        ga[1, 2 * j + 1] = agv[rows, :].astype(BF16)
    ar_start(1)
    pass_on(3)
    ar_one(1)
    add_up(7, partp)
    e2_before.wait_send()
    e2_after.wait_send()
    remote(es.at[0], er.at[1], e2_ss.at[0], e2_rs.at[1], before).wait_recv()
    remote(es.at[1], er.at[0], e2_ss.at[1], e2_rs.at[0], after).wait_recv()
    for half, window in ((0, awk), (1, awv)):
        factor = SCALE if half == 0 else 1.0
        for b in range(QB):
            rows = slice(b * BS, (b + 1) * BS)
            total = window[(b + 1) * BS:(b + 2) * BS, :] * factor + partp[half, rows, :]
            if b == 0:
                total += er[0, half].astype(F32)
            if b == QB - 1:
                total += er[1, half].astype(F32)
            partp[half, rows, :] = total
    ar_two(1)
    ar_three(1)
    ar_end(1)
    for half in range(2):
        p_copy(3, half, True).wait_recv()
        p_copy(3, half, False).wait_recv()
        for b in range(QB):
            rows = slice(b * BS, (b + 1) * BS)
            total = partp[half, rows, :]
            total += srp[3, half, rows, :].astype(F32) + srm[3, half, rows, :].astype(F32)
            for j in range(2):
                total += gall[1, 2 * j + half].astype(F32) * flag(glob[j], blk * QB + b)
            dkvb[half, rows, :] = total.astype(BF16)

    def part_rows(h):
        return pl.ds(pl.multiple_of(h * PART, 32), PART)

    def dkv_copy(h):
        return remote(dkvb.at[:, part_rows(h), :], dkv_out.at[head], dkv_ss.at[h], dkv_rs.at[head], (blk, h))

    def dkv_arrival(h):
        return remote(dkvb.at[:, part_rows(h), :], dkv_out.at[h], dkv_ss.at[h], dkv_rs.at[h], (blk, h))

    own_dkv = pltpu.make_async_copy(dkvb.at[:, mine, :], dkv_out.at[head], loc.at[5])

    def send_dkv(k, c):
        dkv_copy(peer(k)).start()
        return c

    lax.fori_loop(1, NH, send_dkv, 0)
    own_dkv.start()

    def drain(k, c):
        h = (head + k) % NH
        kv_copy(h).wait_send()
        q_copy(h).wait_send()
        g_copy(h).wait_send()
        o_copy(h).wait_send()
        dq_copy(h).wait_send()
        dkv_copy(h).wait_send()
        o_arrival(h).wait_recv()
        dq_arrival(h).wait_recv()
        dkv_arrival(h).wait_recv()
        return c

    for step in range(4):
        for half in range(2):
            if step < 3 or half == 0:
                z_copy(step, half, True).wait_send()
            if step < 3 or half == 1:
                z_copy(step, half, False).wait_send()
            if step > 0 or half == 0:
                p_copy(step, half, True).wait_send()
            if step > 0 or half == 1:
                p_copy(step, half, False).wait_send()
    to_after.wait_send()
    to_before.wait_send()

    def drain_column(dy, c):
        for index in range(8):
            y_copy(dy, index, shard_of(order[index][1])).wait_send()
            w_copy(dy, index).wait_send()
        return c

    lax.fori_loop(1, NY, drain_column, 0)
    ar_drain(0)
    ar_drain(1)
    lax.fori_loop(1, NH, drain, 0)
    own_o.wait()
    own_dq.wait()
    own_dkv.wait()


def tables(rand_blocks, global_blocks):
    blk = lax.axis_index("blk")
    head = lax.axis_index("head")
    y, z = blk // NZ, blk % NZ
    chosen = lax.dynamic_slice_in_dim(rand_blocks, head, 1, 1).reshape(NY, NZ, SLOTS)
    column = lax.dynamic_slice_in_dim(chosen, z, 1, 1)
    owners = y * NZ + jnp.arange(NZ, dtype=jnp.int32)[None, :, None]
    want = jnp.max(jnp.where(column // QB == owners, column % QB, -1), axis=2)
    own = lax.dynamic_slice_in_dim(chosen.reshape(NY * NZ, SLOTS), blk, 1, 0)[0] // QB
    shards = jnp.arange(NY * NZ, dtype=jnp.int32)[:, None]
    slot = jnp.max(
        jnp.where(own[None, :] == shards, jnp.arange(SLOTS, dtype=jnp.int32)[None, :], 0), axis=1
    )
    want = want.reshape(-1)
    picked = jnp.maximum(want, 0)
    shard = global_blocks // QB
    return jnp.concatenate(
        [want, picked, own, slot, global_blocks, global_blocks % QB, shard]
    )


def on_device(queries, keys, values, out_grad, rand_blocks, global_blocks):
    tab = tables(rand_blocks, global_blocks)
    heads = queries.shape[1] // NH
    q_s = queries.reshape(PART, NH, heads, DH).transpose(1, 0, 2, 3).reshape(NH, ROWS, DH)
    g_s = out_grad.reshape(PART, NH, heads, DH).transpose(1, 0, 2, 3).reshape(NH, ROWS, DH)
    kv_s = jnp.stack([keys, values]).transpose(2, 0, 1, 3)
    vm = lambda shape, dtype=BF16: pltpu.VMEM(shape, dtype)
    dma = lambda *shape: pltpu.SemaphoreType.DMA(shape)
    total = NH * ROWS
    pair = (2, BS, DH)
    anywhere = pl.BlockSpec(memory_space=pl.ANY)
    o_h, dq_h, dkv_h = pl.pallas_call(
        body,
        out_shape=(
            jax.ShapeDtypeStruct((NH, ROWS, DH), BF16),
            jax.ShapeDtypeStruct((NH, ROWS, DH), BF16),
            jax.ShapeDtypeStruct((NH, 2, PART, DH), BF16),
        ),
        in_specs=[pl.BlockSpec(memory_space=pltpu.SMEM), anywhere, anywhere, anywhere],
        out_specs=(anywhere, anywhere, anywhere),
        scratch_shapes=[
            vm((total, DH)), vm((total, DH)),
            *[vm((2, ROWS, DH)) for _ in range(8)],
            vm((32,) + pair), vm((32,) + pair), vm((2,) + pair),
            vm((QB, NEAR, DH)), vm((QB, NEAR, DH)), vm((QB, DH, NEAR)), vm((QB, DH, NEAR)),
            vm((QB, FAR, DH)), vm((QB, FAR, DH)), vm((QB, DH, FAR)), vm((QB, DH, FAR)),
            vm((CHUNKS, NEAR, CHUNK)), vm((CHUNKS, FAR, CHUNK)), vm((CHUNKS, DH, CHUNK), F32),
            vm((CHUNKS, 8, CHUNK), F32),
            vm((total, DH)), vm((total, DH)),
            vm(((QB + 2) * BS, DH), F32), vm(((QB + 2) * BS, DH), F32),
            vm((2 * BS, DH), F32), vm((2 * BS, DH), F32),
            vm((SLOTS * BS, DH), F32), vm((SLOTS * BS, DH), F32),
            vm((32,) + pair), vm((32,) + pair), vm((2,) + pair), vm((2,) + pair),
            vm((2, ROWS, DH), F32), vm((2, ROWS, DH), F32),
            *[vm((4, 2, ROWS, DH)) for _ in range(4)],
            vm((2, ROWS, DH)),
            vm((2, NY, BS, DH)), vm((2, NY, BS, DH)), vm((2, BS, DH)), vm((2, NZ, PIECE, DH)),
            vm((2, PIECE, DH)), vm((2, BS, DH)), vm((2, NY, BS, DH)),
            dma(NH), dma(NH), dma(NH), dma(NH), dma(NH), dma(NH), dma(6),
            dma(4, 2), dma(4, 2), dma(4, 2), dma(4, 2), dma(2), dma(2), dma(8, NY), dma(8, NY),
            dma(2, NY), dma(2, NY), dma(2, NZ), dma(2, NZ), dma(2, NZ), dma(2, NZ), dma(2, NY), dma(2, NY),
            dma(NH), dma(NH), dma(NH), dma(NH), dma(8, NY), dma(8, NY), dma(2), dma(2),
            dma(4, 2), dma(4, 2), dma(4, 2), dma(4, 2), dma(NH), dma(NH),
        ],
        compiler_params=pltpu.CompilerParams(
            collective_id=0, has_side_effects=True, vmem_limit_bytes=60 * 2**20
        ),
    )(tab, q_s, g_s, kv_s)

    def rows_back(part):
        return part.reshape(NH, PART, heads, DH).transpose(1, 0, 2, 3).reshape(PART, NH * heads, DH)

    kv_back = dkv_h.transpose(1, 2, 0, 3)
    return rows_back(o_h), rows_back(dq_h), kv_back[0], kv_back[1]


def solution(mesh):
    rows = P(("blk", "head"), None, None)
    return jax.shard_map(
        on_device,
        mesh=mesh,
        in_specs=(rows, rows, rows, rows, P(), P()),
        out_specs=(rows, rows, rows, rows),
        check_vma=False,
    )
```

time: 176 us -> 160 us (0.909)
  Pallas kernels: 161 us -> 145 us
    pallas_call x1, Pallas kernels: 161 us -> 145 us  [on_device(): pl.pallas_call(body, out_shape=(jax.ShapeDtypeStruct((NH, ROWS, DH), BF16...]
where the time goes in v2:
time: 160 us
  Pallas kernels  145 us (91%)
  local copies, waits for them, and re-layouts  12.2 us (8%)
  other arithmetic  1.97 us (1%)
    pallas_call x1, Pallas kernels, on_device(): pl.pallas_call(body, out_shape=(jax.ShapeDtypeStruct((NH, ROWS, DH), BF16...  145 us
    reshape x2, local copies, waits for them, and re-layouts, rows_back(): part.reshape(NH, PART, heads, DH).transpose(1, 0, 2, 3)  4.64 us

profile of v2, /device:TPU:1, one launch (start us, length us, event | category | flops | bytes accessed | tf_op | source)
XLA Modules:
  0.0 160.1 jit_solution(6361694160903811186)
XLA Ops:
  0.6 0.0 copy-start
  0.6 0.0 copy-start.2
  0.7 0.8 and_select_fusion.2
  1.5 0.8 constant_dynamic-slice_fusion.1
  2.3 0.1 copy.28
  2.5 0.1 reshape_reshape.3
  2.6 0.1 reshape.53
  2.7 0.2 select_reduce_fusion
  2.9 0.1 reshape.54
  3.0 0.1 select_reduce_fusion.1
  3.1 1.3 concatenate.3.tab
  4.4 1.1 copy_bitcast_fusion.4
  5.5 0.8 maximum_bitcast_fusion.kv_s
  6.2 0.0 copy-done
  6.2 0.0 copy-done.2
  6.3 2.4 %copy_bitcast_fusion.2 = (bf16[8,768,128]{2,1,0:T(8,128)(2,1)}, bf16[8,768,128]{2,1,0:T(8,128)(2,1)}) fusion(bf16[96,64,128]{2,1,0:T(8,128)(2,1)S(1)} %copy-done, bf16[96,64,128]{2,1,0:T(8,128)(2,1)S(1)} %copy-done.2), kind=kLoop, calls=%fused_computation.2 | loop fusion | bytes 6291456 | tf_op jit(solution)/shard_map/reshape | solution.py:708
  8.7 145.2 %shard_map.93 = (bf16[8,768,128]{2,1,0:T(8,128)(2,1)}, bf16[8,768,128]{2,1,0:T(8,128)(2,1)}, bf16[8,2,96,128]{3,2,1,0:T(8,128)(2,1)}) custom-call(s32[120]{0:T(128)} %concatenate.3.tab, bf16[8,768,128]{2,1,0:T(8,128)(2,1)} %get-tuple-element.34.q_s, bf16[8,768,128]{2,1,0:T(8,128)(2,1)} %get-tuple-element.33.g_s, bf16[8,2,96,128]{3,2,1,0:T(8,128)(2,1)} %maximum_bitcast_fusion.kv_s), custom_call_target="tpu_custom_call" | custom-call | tf_op jit(solution)/shard_map/pallas_call | solution.py:715
  153.9 0.0 copy-start.3
  153.9 3.0 %copy_bitcast_fusion.1 = bf16[96,64,128]{2,1,0:T(8,128)(2,1)} fusion(bf16[8,768,128]{2,1,0:T(8,128)(2,1)} %get-tuple-element.7), kind=kLoop, calls=%fused_computation.1 | loop fusion | bytes 3145728 | tf_op jit(solution)/shard_map/reshape | solution.py:754
  157.0 0.0 copy-done.3
  157.0 0.0 copy-start.1
  157.0 0.8 copy.37
  157.8 0.8 copy.36
  158.5 0.0 copy-done.1
  158.5 1.6 copy_bitcast_fusion
  (6 shorter events, 0.1 us)
Async XLA Ops:
  0.6 5.6 %copy-start = (bf16[96,64,128]{2,1,0:T(8,128)(2,1)S(1)}, bf16[96,64,128]{2,1,0:T(8,128)(2,1)}, u32[]{:S(2)}) copy-start(bf16[96,64,128]{2,1,0:T(8,128)(2,1)} %param.6) | copy-start | bytes 4718596
  0.6 5.6 %copy-start.2 = (bf16[96,64,128]{2,1,0:T(8,128)(2,1)S(1)}, bf16[96,64,128]{2,1,0:T(8,128)(2,1)}, u32[]{:S(2)}) copy-start(bf16[96,64,128]{2,1,0:T(8,128)(2,1)} %param.9) | copy-start | bytes 4718596
  153.9 3.1 %copy-start.3 = (bf16[8,2,96,128]{3,2,1,0:T(8,128)(2,1)S(1)}, bf16[8,2,96,128]{3,2,1,0:T(8,128)(2,1)}, u32[]{:S(2)}) copy-start(bf16[8,2,96,128]{3,2,1,0:T(8,128)(2,1)} %get-tuple-element.9) | copy-start | bytes 1179652
  157.0 1.5 copy-start.1

commit v3 on v2

--- a/solution.py
+++ b/solution.py
@@ -39,7 +39,7 @@
     qh, gh, r0, rp1, rp2, rp3, rm1, rm2, rm3, r4, xs, xr, edge,
     lkn, lvn, lktn, lvtn, lkf, lvf, lktf, lvtf, exn, dsf, o1, stats, ob, dqb,
     awk, awv, agk, agv, ark, arv,
-    ys, yr, es, er, partp, partm, ssp, ssm, srp, srm, dkvb,
+    ys, yr, es, er, partp, partm, fin, ssp, ssm, srp, srm, dkvb,
     ga, gy, gp, gz, gm, gf, gall,
     head_ss, head_rs, q_ss, q_rs, g_ss, g_rs, loc,
     zp_ss, zp_rs, zm_ss, zm_rs, e_ss, e_rs, y_ss, y_rs,
@@ -135,11 +135,6 @@
         return c
 
     lax.fori_loop(1, NH, send_kv, 0)
-    own_q.start()
-    own_g.start()
-    lax.fori_loop(1, NH, send_q, 0)
-    lax.fori_loop(1, NH, send_g, 0)
-
     zero = jnp.zeros((BS, DH), F32)
     for ref in (awk, awv, agk, agv, ark, arv):
         def clear(n, c, ref=ref):
@@ -173,6 +168,10 @@
         z_copy(0, half, False).start()
     to_after.start()
     to_before.start()
+    own_q.start()
+    own_g.start()
+    lax.fori_loop(1, NH, send_q, 0)
+    lax.fori_loop(1, NH, send_g, 0)
 
     glob = [tab[T_GLOB + j] for j in range(2)]
     g_within = [tab[T_GLOB + 2 + j] for j in range(2)]
@@ -292,70 +291,78 @@
             if 0 <= e - s < QB:
                 place(e - s, s, kb, vb)
 
-    def attend_near(j):
-        rows = pl.ds(pl.multiple_of(j * CHUNK, CHUNK), CHUNK)
-        i = j // 4
-        q = qh[rows, :]
-        st = dot(lkn[i], q, ((1,), (1,)))
-        peak = jnp.max(st, axis=0, keepdims=True)
-        ex = jnp.exp2((st - peak) * (SCALE * LOG2E))
-        stats[j, 0:1, :] = peak
-        stats[j, 1:2, :] = jnp.sum(ex, axis=0, keepdims=True)
-        eb = ex.astype(BF16)
-        exn[j] = eb
-        o1[j] = dot(lvtn[i], eb, ((1,), (0,)))
-
-    def attend_far(j):
-        rows = pl.ds(pl.multiple_of(j * CHUNK, CHUNK), CHUNK)
-        i = j // 4
-        q = qh[rows, :]
-        g = gh[rows, :]
-        st = dot(lkf[i], q, ((1,), (1,)))
-        dpt = dot(lvf[i], g, ((1,), (1,)))
-        gt = g.astype(F32).T
-        before_peak = stats[j, 0:1, :]
-        peak = jnp.maximum(before_peak, jnp.max(st, axis=0, keepdims=True))
-        shrink = jnp.exp2((before_peak - peak) * (SCALE * LOG2E))
-        ex = jnp.exp2((st - peak) * (SCALE * LOG2E))
-        inv = 1.0 / (shrink * stats[j, 1:2, :] + jnp.sum(ex, axis=0, keepdims=True))
-        near = shrink * inv
-        pt = ex * inv
-        pb = pt.astype(BF16)
-        ot = o1[j] * near + dot(lvtf[i], pb, ((1,), (0,)))
-        ob[rows, :] = ot.T.astype(BF16)
-        delta = jnp.sum(ot.astype(BF16).astype(F32) * gt, axis=0, keepdims=True)
-        stats[j, 2:3, :] = near
-        stats[j, 3:4, :] = delta
-        ds = (pt * (dpt - delta)).astype(BF16)
-        dsf[j] = ds
-        rbase = pl.multiple_of(i * FAR, BS)
-        arv[pl.ds(rbase, FAR), :] += dot(pb, g, ((1,), (0,)))
-        ark[pl.ds(rbase, FAR), :] += dot(ds, q, ((1,), (0,)))
-
-    def attend_back(j):
-        rows = pl.ds(pl.multiple_of(j * CHUNK, CHUNK), CHUNK)
-        i = j // 4
-        q = qh[rows, :]
-        g = gh[rows, :]
-        dpt = dot(lvn[i], g, ((1,), (1,)))
-        pt = exn[j].astype(F32) * stats[j, 2:3, :]
-        pb = pt.astype(BF16)
-        ds = (pt * (dpt - stats[j, 3:4, :])).astype(BF16)
-        dqt = dot(lktn[i], ds, ((1,), (0,))) + dot(lktf[i], dsf[j], ((1,), (0,)))
-        dqb[rows, :] = (dqt * SCALE).T.astype(BF16)
-        dv = dot(pb, g, ((1,), (0,)))
-        dk = dot(ds, q, ((1,), (0,)))
-        base = pl.multiple_of(i * BS, BS)
-        awk[pl.ds(base, 3 * BS), :] += dk[0:3 * BS]
-        awv[pl.ds(base, 3 * BS), :] += dv[0:3 * BS]
-        agk[...] += dk[3 * BS:]
-        agv[...] += dv[3 * BS:]
-
-    def three(h, what):
-        def chunk(t, c):
-            what(h * 3 + t)
-            return c
-        lax.fori_loop(0, 3, chunk, 0)
+    def chunks_of(h):
+        js = [h * 3 + t for t in range(3)]
+        return js, [j // 4 for j in js], [pl.ds(pl.multiple_of(j * CHUNK, CHUNK), CHUNK) for j in js]
+
+    turns = range(3)
+    nt, nn = ((1,), (1,)), ((1,), (0,))
+
+    def attend_near(h):
+        js, at, rows = chunks_of(h)
+        st = [dot(lkn[at[t]], qh[rows[t], :], nt) for t in turns]
+        peak = [jnp.max(v, axis=0, keepdims=True) for v in st]
+        ex = [jnp.exp2((st[t] - peak[t]) * (SCALE * LOG2E)) for t in turns]
+        total = [jnp.sum(v, axis=0, keepdims=True) for v in ex]
+        eb = [v.astype(BF16) for v in ex]
+        ot = [dot(lvtn[at[t]], eb[t], nn) for t in turns]
+        for t in turns:
+            exn[js[t]] = eb[t]
+            o1[js[t]] = ot[t]
+            stats[js[t], 0:1, :] = peak[t]
+            stats[js[t], 1:2, :] = total[t]
+
+    def attend_far(h):
+        js, at, rows = chunks_of(h)
+        q = [qh[r, :] for r in rows]
+        g = [gh[r, :] for r in rows]
+        first = [stats[j, 0:1, :] for j in js]
+        first_total = [stats[j, 1:2, :] for j in js]
+        first_out = [o1[j] for j in js]
+        st = [dot(lkf[at[t]], q[t], nt) for t in turns]
+        dpt = [dot(lvf[at[t]], g[t], nt) for t in turns]
+        gt = [v.astype(F32).T for v in g]
+        peak = [jnp.maximum(first[t], jnp.max(st[t], axis=0, keepdims=True)) for t in turns]
+        shrink = [jnp.exp2((first[t] - peak[t]) * (SCALE * LOG2E)) for t in turns]
+        ex = [jnp.exp2((st[t] - peak[t]) * (SCALE * LOG2E)) for t in turns]
+        inv = [1.0 / (shrink[t] * first_total[t] + jnp.sum(ex[t], axis=0, keepdims=True)) for t in turns]
+        near = [shrink[t] * inv[t] for t in turns]
+        pt = [ex[t] * inv[t] for t in turns]
+        pb = [v.astype(BF16) for v in pt]
+        ot = [first_out[t] * near[t] + dot(lvtf[at[t]], pb[t], nn) for t in turns]
+        delta = [jnp.sum(ot[t].astype(BF16).astype(F32) * gt[t], axis=0, keepdims=True) for t in turns]
+        ds = [(pt[t] * (dpt[t] - delta[t])).astype(BF16) for t in turns]
+        dv = [dot(pb[t], g[t], nn) for t in turns]
+        dk = [dot(ds[t], q[t], nn) for t in turns]
+        for t in turns:
+            ob[rows[t], :] = ot[t].T.astype(BF16)
+            stats[js[t], 2:3, :] = near[t]
+            stats[js[t], 3:4, :] = delta[t]
+            dsf[js[t]] = ds[t]
+        for t in turns:
+            rbase = pl.ds(pl.multiple_of(at[t] * FAR, BS), FAR)
+            arv[rbase, :] += dv[t]
+            ark[rbase, :] += dk[t]
+
+    def attend_back(h):
+        js, at, rows = chunks_of(h)
+        q = [qh[r, :] for r in rows]
+        g = [gh[r, :] for r in rows]
+        dpt = [dot(lvn[at[t]], g[t], nt) for t in turns]
+        pt = [exn[js[t]].astype(F32) * stats[js[t], 2:3, :] for t in turns]
+        pb = [v.astype(BF16) for v in pt]
+        ds = [(pt[t] * (dpt[t] - stats[js[t], 3:4, :])).astype(BF16) for t in turns]
+        dqt = [dot(lktn[at[t]], ds[t], nn) + dot(lktf[at[t]], dsf[js[t]], nn) for t in turns]
+        dv = [dot(pb[t], g[t], nn) for t in turns]
+        dk = [dot(ds[t], q[t], nn) for t in turns]
+        for t in turns:
+            dqb[rows[t], :] = (dqt[t] * SCALE).T.astype(BF16)
+        for t in turns:
+            base = pl.ds(pl.multiple_of(at[t] * BS, BS), 3 * BS)
+            awk[base, :] += dk[t][0:3 * BS]
+            awv[base, :] += dv[t][0:3 * BS]
+        agk[...] += dk[0][3 * BS:] + dk[1][3 * BS:] + dk[2][3 * BS:]
+        agv[...] += dv[0][3 * BS:] + dv[1][3 * BS:] + dv[2][3 * BS:]
 
     def near_parts(first, last):
         def part(k, c):
@@ -365,7 +372,7 @@
             def _():
                 q_arrival(h).wait_recv()
 
-            three(h, attend_near)
+            attend_near(h)
             return c
 
         lax.fori_loop(first, last, part, 0)
@@ -462,7 +469,7 @@
     def far_part(n, c):
         k = NH - 1 - n
         h = peer(k)
-        three(h, attend_far)
+        attend_far(h)
 
         @pl.when(k > 0)
         def _():
@@ -477,7 +484,7 @@
         def part(n, c):
             k = NH - 1 - n
             h = peer(k)
-            three(h, attend_back)
+            attend_back(h)
 
             @pl.when(k > 0)
             def _():
@@ -504,17 +511,17 @@
     def slot_rows(slot):
         return pl.ds(slot * BS, BS)
 
-    for index, delta in enumerate(back):
-        sz = shard_of(delta)
-
-        def give(dy, c, index=index, sz=sz):
+    def give(index):
+        sz = shard_of(back[index])
+
+        def one(dy, c):
             slot = tab[T_SLOT + ((y + dy) % NY) * NZ + sz]
             ys[index * 4 + dy, 0] = (ark[slot_rows(slot), :] * SCALE).astype(BF16)
             ys[index * 4 + dy, 1] = arv[slot_rows(slot), :].astype(BF16)
             w_copy(dy, index).start()
             return c
 
-        lax.fori_loop(1, NY, give, 0)
+        lax.fori_loop(1, NY, one, 0)
         slot = tab[T_SLOT + y * NZ + sz]
         yr[index * 4 + y, 0] = (ark[slot_rows(slot), :] * SCALE).astype(BF16)
         yr[index * 4 + y, 1] = arv[slot_rows(slot), :].astype(BF16)
@@ -531,9 +538,9 @@
 
         def one_block(b, c):
             for half in range(2):
-                total = yr[index * 4, half].astype(F32) * flag(hits[0], b)
+                total = yr[index * 4, half].astype(part.dtype) * flag(hits[0], b).astype(part.dtype)
                 for yy in range(1, NY):
-                    total += yr[index * 4 + yy, half].astype(F32) * flag(hits[yy], b)
+                    total += yr[index * 4 + yy, half].astype(part.dtype) * flag(hits[yy], b).astype(part.dtype)
                 part[half, pl.ds(pl.multiple_of(b * BS, BS), BS), :] = total
             return c
 
@@ -552,30 +559,33 @@
                 for half in (first, 1 - first):
                     if waits != (step > 1 or half == first):
                         continue
-                    total = part[half]
+                    total = part[half].astype(F32)
                     if waits:
                         p_copy(step - 1, half, upward).wait_recv()
                         total += recv[step - 1, half].astype(F32)
                     send[step, half] = total.astype(BF16)
                     p_copy(step, half, upward).start()
 
+    give(0)
+    give(1)
+    give(2)
     back_parts(0, 2)
     add_up(0, partp)
     ssp[0, 0] = partp[0].astype(BF16)
     p_copy(0, 0, True).start()
     ssm[0, 1] = partp[1].astype(BF16)
     p_copy(0, 1, False).start()
-    back_parts(2, 4)
+    give(3)
+    give(4)
     add_up(1, partp)
     add_up(2, partm)
+    back_parts(2, 4)
     pass_on(1)
+    give(5)
+    give(6)
     add_up(3, partp)
     add_up(4, partm)
-    back_parts(4, 7)
-    pass_on(2)
-    add_up(5, partp)
-    add_up(6, partm)
-    back_parts(7, 8)
+    back_parts(4, 8)
     own_dq.start()
     for n, at in ((0, 0), (1, QB + 1)):
         rows = slice(at * BS, (at + 1) * BS)
@@ -590,9 +600,14 @@
         ga[1, 2 * j] = (agk[rows, :] * SCALE).astype(BF16)
         ga[1, 2 * j + 1] = agv[rows, :].astype(BF16)
     ar_start(1)
+    pass_on(2)
+    give(7)
+    ar_one(1)
+    add_up(5, partp)
+    add_up(6, partm)
     pass_on(3)
-    ar_one(1)
-    add_up(7, partp)
+    ar_two(1)
+    add_up(7, fin)
     e2_before.wait_send()
     e2_after.wait_send()
     remote(es.at[0], er.at[1], e2_ss.at[0], e2_rs.at[1], before).wait_recv()
@@ -601,13 +616,12 @@
         factor = SCALE if half == 0 else 1.0
         for b in range(QB):
             rows = slice(b * BS, (b + 1) * BS)
-            total = window[(b + 1) * BS:(b + 2) * BS, :] * factor + partp[half, rows, :]
+            total = window[(b + 1) * BS:(b + 2) * BS, :] * factor + fin[half, rows, :]
             if b == 0:
                 total += er[0, half].astype(F32)
             if b == QB - 1:
                 total += er[1, half].astype(F32)
-            partp[half, rows, :] = total
-    ar_two(1)
+            fin[half, rows, :] = total
     ar_three(1)
     ar_end(1)
     for half in range(2):
@@ -615,7 +629,7 @@
         p_copy(3, half, False).wait_recv()
         for b in range(QB):
             rows = slice(b * BS, (b + 1) * BS)
-            total = partp[half, rows, :]
+            total = fin[half, rows, :]
             total += srp[3, half, rows, :].astype(F32) + srm[3, half, rows, :].astype(F32)
             for j in range(2):
                 total += gall[1, 2 * j + half].astype(F32) * flag(glob[j], blk * QB + b)
@@ -734,7 +748,7 @@
             vm((2 * BS, DH), F32), vm((2 * BS, DH), F32),
             vm((SLOTS * BS, DH), F32), vm((SLOTS * BS, DH), F32),
             vm((32,) + pair), vm((32,) + pair), vm((2,) + pair), vm((2,) + pair),
-            vm((2, ROWS, DH), F32), vm((2, ROWS, DH), F32),
+            vm((2, ROWS, DH)), vm((2, ROWS, DH)), vm((2, ROWS, DH), F32),
             *[vm((4, 2, ROWS, DH)) for _ in range(4)],
             vm((2, ROWS, DH)),
             vm((2, NY, BS, DH)), vm((2, NY, BS, DH)), vm((2, BS, DH)), vm((2, NZ, PIECE, DH)),

time: 160 us -> 143 us (0.89)
  Pallas kernels: 145 us -> 127 us
    pallas_call x1, Pallas kernels: 145 us -> 127 us  [on_device(): pl.pallas_call(body, out_shape=(jax.ShapeDtypeStruct((NH, ROWS, DH), BF16...]
where the time goes in v3:
time: 143 us; the launch traced here: 142 us
  Pallas kernels  127 us (89%)
  local copies, waits for them, and re-layouts  12.2 us (9%)
  other arithmetic  1.97 us (1%)
    pallas_call x1, Pallas kernels, on_device(): pl.pallas_call(body, out_shape=(jax.ShapeDtypeStruct((NH, ROWS, DH), BF16...  127 us
    reshape x2, local copies, waits for them, and re-layouts, rows_back(): part.reshape(NH, PART, heads, DH).transpose(1, 0, 2, 3)  4.64 us

profile of v3, /device:TPU:1, one launch (start us, length us, event | category | flops | bytes accessed | tf_op | source)
XLA Modules:
  0.0 142.2 jit_solution(16078182655986761144)
XLA Ops:
  0.6 0.0 copy-start
  0.6 0.0 copy-start.2
  0.7 0.8 and_select_fusion.2
  1.5 0.8 constant_dynamic-slice_fusion.1
  2.3 0.1 copy.28
  2.5 0.1 reshape_reshape.3
  2.6 0.1 reshape.53
  2.7 0.2 select_reduce_fusion
  2.9 0.1 reshape.54
  3.0 0.1 select_reduce_fusion.1
  3.1 1.3 concatenate.3.tab
  4.4 1.1 copy_bitcast_fusion.4
  5.5 0.8 maximum_bitcast_fusion.kv_s
  6.2 0.0 copy-done
  6.2 0.0 copy-done.2
  6.3 2.4 %copy_bitcast_fusion.2 = (bf16[8,768,128]{2,1,0:T(8,128)(2,1)}, bf16[8,768,128]{2,1,0:T(8,128)(2,1)}) fusion(bf16[96,64,128]{2,1,0:T(8,128)(2,1)S(1)} %copy-done, bf16[96,64,128]{2,1,0:T(8,128)(2,1)S(1)} %copy-done.2), kind=kLoop, calls=%fused_computation.2 | loop fusion | bytes 6291456 | tf_op jit(solution)/shard_map/reshape | solution.py:722
  8.7 127.4 %shard_map.93 = (bf16[8,768,128]{2,1,0:T(8,128)(2,1)}, bf16[8,768,128]{2,1,0:T(8,128)(2,1)}, bf16[8,2,96,128]{3,2,1,0:T(8,128)(2,1)}) custom-call(s32[120]{0:T(128)} %concatenate.3.tab, bf16[8,768,128]{2,1,0:T(8,128)(2,1)} %get-tuple-element.34.q_s, bf16[8,768,128]{2,1,0:T(8,128)(2,1)} %get-tuple-element.33.g_s, bf16[8,2,96,128]{3,2,1,0:T(8,128)(2,1)} %maximum_bitcast_fusion.kv_s), custom_call_target="tpu_custom_call" | custom-call | tf_op jit(solution)/shard_map/pallas_call | solution.py:729
  136.1 0.0 copy-start.3
  136.1 3.0 %copy_bitcast_fusion.1 = bf16[96,64,128]{2,1,0:T(8,128)(2,1)} fusion(bf16[8,768,128]{2,1,0:T(8,128)(2,1)} %get-tuple-element.7), kind=kLoop, calls=%fused_computation.1 | loop fusion | bytes 3145728 | tf_op jit(solution)/shard_map/reshape | solution.py:768
  139.1 0.0 copy-done.3
  139.1 0.0 copy-start.1
  139.1 0.8 copy.37
  139.9 0.8 copy.36
  140.7 0.0 copy-done.1
  140.7 1.6 %copy_bitcast_fusion = bf16[96,64,128]{2,1,0:T(8,128)(2,1)} fusion(bf16[8,768,128]{2,1,0:T(8,128)(2,1)S(1)} %copy-done.1), kind=kLoop, calls=%fused_computation | loop fusion | bytes 3145728 | tf_op jit(solution)/shard_map/reshape | solution.py:768
  (6 shorter events, 0.1 us)
Async XLA Ops:
  0.6 5.6 %copy-start = (bf16[96,64,128]{2,1,0:T(8,128)(2,1)S(1)}, bf16[96,64,128]{2,1,0:T(8,128)(2,1)}, u32[]{:S(2)}) copy-start(bf16[96,64,128]{2,1,0:T(8,128)(2,1)} %param.6) | copy-start | bytes 4718596
  0.6 5.6 %copy-start.2 = (bf16[96,64,128]{2,1,0:T(8,128)(2,1)S(1)}, bf16[96,64,128]{2,1,0:T(8,128)(2,1)}, u32[]{:S(2)}) copy-start(bf16[96,64,128]{2,1,0:T(8,128)(2,1)} %param.9) | copy-start | bytes 4718596
  136.1 3.1 %copy-start.3 = (bf16[8,2,96,128]{3,2,1,0:T(8,128)(2,1)S(1)}, bf16[8,2,96,128]{3,2,1,0:T(8,128)(2,1)}, u32[]{:S(2)}) copy-start(bf16[8,2,96,128]{3,2,1,0:T(8,128)(2,1)} %get-tuple-element.9) | copy-start | bytes 1179652
  139.1 1.5 %copy-start.1 = (bf16[8,768,128]{2,1,0:T(8,128)(2,1)S(1)}, bf16[8,768,128]{2,1,0:T(8,128)(2,1)}, u32[]{:S(2)}) copy-start(bf16[8,768,128]{2,1,0:T(8,128)(2,1)} %get-tuple-element.8) | copy-start | bytes 4718596

commit v4 on v3

--- a/solution.py
+++ b/solution.py
@@ -35,12 +35,12 @@
 
 
 def body(
-    tab, q_s, g_s, kv_s, o_out, dq_out, dkv_out,
+    tab, q_in, g_in, kv_s, o_out, dq_out, dkv_out,
     qh, gh, r0, rp1, rp2, rp3, rm1, rm2, rm3, r4, xs, xr, edge,
     lkn, lvn, lktn, lvtn, lkf, lvf, lktf, lvtf, exn, dsf, o1, stats, ob, dqb,
     awk, awv, agk, agv, ark, arv,
     ys, yr, es, er, partp, partm, fin, ssp, ssm, srp, srm, dkvb,
-    ga, gy, gp, gz, gm, gf, gall,
+    ga, gy, gp, gz, gm, gf, gall, raw,
     head_ss, head_rs, q_ss, q_rs, g_ss, g_rs, loc,
     zp_ss, zp_rs, zm_ss, zm_rs, e_ss, e_rs, y_ss, y_rs,
     a0_ss, a0_rs, a1_ss, a1_rs, a2_ss, a2_rs, a3_ss, a3_rs,
@@ -71,6 +71,9 @@
             src_ref=src, dst_ref=dst, send_sem=ss, recv_sem=rs, device_id=dev, device_id_type=MESH
         )
 
+    raw_q = pltpu.make_async_copy(q_in, raw, loc.at[6])
+    raw_g = pltpu.make_async_copy(g_in, raw, loc.at[7])
+    raw_q.start()
     bar = pltpu.get_barrier_semaphore()
 
     def greet(dev):
@@ -96,34 +99,45 @@
     mine = pl.ds(pl.multiple_of(head * PART, 32), PART)
     rows_mine = pl.ds(pl.multiple_of(head * ROWS, 256), ROWS)
 
-    def kv_copy(h):
-        return remote(kv_s.at[h], r0.at[:, mine, :], head_ss.at[h], head_rs.at[head], (blk, h))
-
-    def kv_arrival(h):
+    def there_rows(h):
+        return pl.ds(pl.multiple_of(h * ROWS, 256), ROWS)
+
+    def kv_copy(h, half):
+        return remote(
+            kv_s.at[h, half], r0.at[half, mine, :], head_ss.at[half, h], head_rs.at[half, head], (blk, h)
+        )
+
+    def kv_arrival(h, half):
         there = pl.ds(pl.multiple_of(h * PART, 32), PART)
-        return remote(kv_s.at[h], r0.at[:, there, :], head_ss.at[h], head_rs.at[h], (blk, h))
+        return remote(
+            kv_s.at[h, half], r0.at[half, there, :], head_ss.at[half, h], head_rs.at[half, h], (blk, h)
+        )
 
     def q_copy(h):
-        return remote(q_s.at[h], qh.at[rows_mine, :], q_ss.at[h], q_rs.at[head], (blk, h))
+        return remote(ob.at[there_rows(h), :], qh.at[rows_mine, :], q_ss.at[h], q_rs.at[head], (blk, h))
 
     def g_copy(h):
-        return remote(g_s.at[h], gh.at[rows_mine, :], g_ss.at[h], g_rs.at[head], (blk, h))
+        return remote(dqb.at[there_rows(h), :], gh.at[rows_mine, :], g_ss.at[h], g_rs.at[head], (blk, h))
 
     def q_arrival(h):
         there = pl.ds(pl.multiple_of(h * ROWS, 256), ROWS)
-        return remote(q_s.at[h], qh.at[there, :], q_ss.at[h], q_rs.at[h], (blk, h))
+        return remote(ob.at[there_rows(h), :], qh.at[there, :], q_ss.at[h], q_rs.at[h], (blk, h))
 
     def g_arrival(h):
         there = pl.ds(pl.multiple_of(h * ROWS, 256), ROWS)
-        return remote(g_s.at[h], gh.at[there, :], g_ss.at[h], g_rs.at[h], (blk, h))
+        return remote(dqb.at[there_rows(h), :], gh.at[there, :], g_ss.at[h], g_rs.at[h], (blk, h))
 
     own_kv = pltpu.make_async_copy(kv_s.at[head], r0.at[:, mine, :], loc.at[0])
-    own_q = pltpu.make_async_copy(q_s.at[head], qh.at[rows_mine, :], loc.at[1])
-    own_g = pltpu.make_async_copy(g_s.at[head], gh.at[rows_mine, :], loc.at[2])
+    own_q = pltpu.make_async_copy(ob.at[rows_mine, :], qh.at[rows_mine, :], loc.at[1])
+    own_g = pltpu.make_async_copy(dqb.at[rows_mine, :], gh.at[rows_mine, :], loc.at[2])
     own_kv.start()
 
-    def send_kv(k, c):
-        kv_copy(peer(k)).start()
+    def send_k(k, c):
+        kv_copy(peer(k), 0).start()
+        return c
+
+    def send_v(k, c):
+        kv_copy(peer(k), 1).start()
         return c
 
     def send_q(k, c):
@@ -134,7 +148,17 @@
         g_copy(peer(k)).start()
         return c
 
-    lax.fori_loop(1, NH, send_kv, 0)
+    lax.fori_loop(1, NH, send_k, 0)
+    lax.fori_loop(1, NH, send_v, 0)
+
+    def regroup(dst):
+        for h in range(NH):
+            rows = raw[:, h * NH:(h + 1) * NH, :].astype(F32).reshape(ROWS, DH)
+            dst[h * ROWS:(h + 1) * ROWS, :] = rows.astype(BF16)
+
+    raw_q.wait()
+    regroup(ob)
+    raw_g.start()
     zero = jnp.zeros((BS, DH), F32)
     for ref in (awk, awv, agk, agv, ark, arv):
         def clear(n, c, ref=ref):
@@ -144,11 +168,11 @@
 
     own_kv.wait()
 
-    def wait_kv(k, c):
-        kv_arrival((head + k) % NH).wait_recv()
-        return c
-
-    lax.fori_loop(1, NH, wait_kv, 0)
+    def wait_kv(half):
+        def one(k, c):
+            kv_arrival((head + k) % NH, half).wait_recv()
+            return c
+        lax.fori_loop(1, NH, one, 0)
 
     plus = [r0, rp1, rp2, rp3, r4]
     minus = [r0, rm1, rm2, rm3, r4]
@@ -164,14 +188,14 @@
     to_after = remote(r0.at[:, pl.ds(ROWS - BS, BS), :], edge.at[0], e_ss.at[0], e_rs.at[0], after)
     to_before = remote(r0.at[:, pl.ds(0, BS), :], edge.at[1], e_ss.at[1], e_rs.at[1], before)
     for half in (0, 1):
+        wait_kv(half)
         z_copy(0, half, True).start()
         z_copy(0, half, False).start()
+        if half == 0:
+            own_q.start()
+            lax.fori_loop(1, NH, send_q, 0)
     to_after.start()
     to_before.start()
-    own_q.start()
-    own_g.start()
-    lax.fori_loop(1, NH, send_q, 0)
-    lax.fori_loop(1, NH, send_g, 0)
 
     glob = [tab[T_GLOB + j] for j in range(2)]
     g_within = [tab[T_GLOB + 2 + j] for j in range(2)]
@@ -384,6 +408,8 @@
             ga[0, 2 * j + half] = (picked * here).astype(BF16)
     ar_start(0)
     serve(0)
+    raw_g.wait()
+    regroup(dqb)
     for e in range(1, QB + 1):
         place_window(e, r0[0, (e - 1) * BS:e * BS, :], r0[1, (e - 1) * BS:e * BS, :])
     ar_one(0)
@@ -397,35 +423,36 @@
             z_copy(step, half, False).start()
 
     forward(1, 0)
-    ar_two(0)
     to_after.wait_recv()
     to_before.wait_recv()
     place_window(0, edge[0, 0], edge[0, 1])
     place_window(QB + 1, edge[1, 0], edge[1, 1])
+    ar_two(0)
     forward(1, 1)
+    own_g.start()
+    lax.fori_loop(1, NH, send_g, 0)
     serve(1)
     serve(2)
+    forward(2, 0)
     ar_three(0)
-    forward(2, 0)
+    forward(2, 1)
+    serve(3)
+    serve(4)
     ar_end(0)
     for j in range(2):
         for i in range(QB):
             place(i, 3 + j, gall[0, 2 * j], gall[0, 2 * j + 1])
-    forward(2, 1)
-    serve(3)
-    serve(4)
     own_q.wait()
+    forward(3, 0)
     near_parts(0, 2)
-    forward(3, 0)
-    near_parts(2, 4)
     forward(3, 1)
     serve(5)
     serve(6)
-    near_parts(4, 6)
+    near_parts(2, 4)
     z_copy(3, 0, True).wait_recv()
     z_copy(3, 1, False).wait_recv()
     serve(7)
-    near_parts(6, 8)
+    near_parts(4, 8)
 
     for index in range(8):
         def wait_y(dy, c, index=index):
@@ -448,9 +475,6 @@
 
     lax.fori_loop(1, NH, wait_g, 0)
 
-    def there_rows(h):
-        return pl.ds(pl.multiple_of(h * ROWS, 256), ROWS)
-
     def o_copy(h):
         return remote(ob.at[there_rows(h), :], o_out.at[head], o_ss.at[h], o_rs.at[head], (blk, h))
 
@@ -477,6 +501,13 @@
 
         return c
 
+    def staging_free(k, c):
+        h = peer(k)
+        q_copy(h).wait_send()
+        g_copy(h).wait_send()
+        return c
+
+    lax.fori_loop(1, NH, staging_free, 0)
     lax.fori_loop(0, NH, far_part, 0)
     own_o.start()
 
@@ -552,24 +583,20 @@
         return remote(ssm.at[step, half], srm.at[step, half], pm_ss.at[step, half], pm_rs.at[step, half], down)
 
     def pass_on(step):
-        for waits in (False, True):
-            for upward in (True, False):
+        for half in (0, 1):
+            for upward in (half == 1, half == 0):
                 send, recv, part = (ssp, srp, partp) if upward else (ssm, srm, partm)
-                first = 0 if upward else 1
-                for half in (first, 1 - first):
-                    if waits != (step > 1 or half == first):
-                        continue
-                    total = part[half].astype(F32)
-                    if waits:
-                        p_copy(step - 1, half, upward).wait_recv()
-                        total += recv[step - 1, half].astype(F32)
-                    send[step, half] = total.astype(BF16)
-                    p_copy(step, half, upward).start()
+                total = part[half].astype(F32)
+                if step > 1 or half == (0 if upward else 1):
+                    p_copy(step - 1, half, upward).wait_recv()
+                    total += recv[step - 1, half].astype(F32)
+                send[step, half] = total.astype(BF16)
+                p_copy(step, half, upward).start()
 
     give(0)
     give(1)
     give(2)
-    back_parts(0, 2)
+    back_parts(0, 4)
     add_up(0, partp)
     ssp[0, 0] = partp[0].astype(BF16)
     p_copy(0, 0, True).start()
@@ -579,12 +606,6 @@
     give(4)
     add_up(1, partp)
     add_up(2, partm)
-    back_parts(2, 4)
-    pass_on(1)
-    give(5)
-    give(6)
-    add_up(3, partp)
-    add_up(4, partm)
     back_parts(4, 8)
     own_dq.start()
     for n, at in ((0, 0), (1, QB + 1)):
@@ -600,13 +621,19 @@
         ga[1, 2 * j] = (agk[rows, :] * SCALE).astype(BF16)
         ga[1, 2 * j + 1] = agv[rows, :].astype(BF16)
     ar_start(1)
+    pass_on(1)
+    give(5)
+    give(6)
+    ar_one(1)
+    add_up(3, partp)
+    add_up(4, partm)
     pass_on(2)
     give(7)
-    ar_one(1)
+    ar_two(1)
     add_up(5, partp)
     add_up(6, partm)
     pass_on(3)
-    ar_two(1)
+    ar_three(1)
     add_up(7, fin)
     e2_before.wait_send()
     e2_after.wait_send()
@@ -622,7 +649,28 @@
             if b == QB - 1:
                 total += er[1, half].astype(F32)
             fin[half, rows, :] = total
-    ar_three(1)
+    def part_rows(h):
+        return pl.ds(pl.multiple_of(h * PART, 32), PART)
+
+    def dkv_copy(h, half):
+        return remote(
+            dkvb.at[half, part_rows(h), :], dkv_out.at[head, half],
+            dkv_ss.at[half, h], dkv_rs.at[half, head], (blk, h),
+        )
+
+    def dkv_arrival(h, half):
+        return remote(
+            dkvb.at[half, part_rows(h), :], dkv_out.at[h, half],
+            dkv_ss.at[half, h], dkv_rs.at[half, h], (blk, h),
+        )
+
+    def own_dkv(half):
+        return pltpu.make_async_copy(dkvb.at[half, mine, :], dkv_out.at[head, half], loc.at[0 if half else 5])
+
+    def send_dkv(half, k, c):
+        dkv_copy(peer(k), half).start()
+        return c
+
     ar_end(1)
     for half in range(2):
         p_copy(3, half, True).wait_recv()
@@ -634,36 +682,21 @@
             for j in range(2):
                 total += gall[1, 2 * j + half].astype(F32) * flag(glob[j], blk * QB + b)
             dkvb[half, rows, :] = total.astype(BF16)
-
-    def part_rows(h):
-        return pl.ds(pl.multiple_of(h * PART, 32), PART)
-
-    def dkv_copy(h):
-        return remote(dkvb.at[:, part_rows(h), :], dkv_out.at[head], dkv_ss.at[h], dkv_rs.at[head], (blk, h))
-
-    def dkv_arrival(h):
-        return remote(dkvb.at[:, part_rows(h), :], dkv_out.at[h], dkv_ss.at[h], dkv_rs.at[h], (blk, h))
-
-    own_dkv = pltpu.make_async_copy(dkvb.at[:, mine, :], dkv_out.at[head], loc.at[5])
-
-    def send_dkv(k, c):
-        dkv_copy(peer(k)).start()
-        return c
-
-    lax.fori_loop(1, NH, send_dkv, 0)
-    own_dkv.start()
+        own_dkv(half).start()
+        lax.fori_loop(1, NH, functools.partial(send_dkv, half), 0)
 
     def drain(k, c):
         h = (head + k) % NH
-        kv_copy(h).wait_send()
-        q_copy(h).wait_send()
-        g_copy(h).wait_send()
+        kv_copy(h, 0).wait_send()
+        kv_copy(h, 1).wait_send()
         o_copy(h).wait_send()
         dq_copy(h).wait_send()
-        dkv_copy(h).wait_send()
+        dkv_copy(h, 0).wait_send()
+        dkv_copy(h, 1).wait_send()
         o_arrival(h).wait_recv()
         dq_arrival(h).wait_recv()
-        dkv_arrival(h).wait_recv()
+        dkv_arrival(h, 0).wait_recv()
+        dkv_arrival(h, 1).wait_recv()
         return c
 
     for step in range(4):
@@ -691,7 +724,8 @@
     lax.fori_loop(1, NH, drain, 0)
     own_o.wait()
     own_dq.wait()
-    own_dkv.wait()
+    own_dkv(0).wait()
+    own_dkv(1).wait()
 
 
 def tables(rand_blocks, global_blocks):
@@ -718,8 +752,6 @@
 def on_device(queries, keys, values, out_grad, rand_blocks, global_blocks):
     tab = tables(rand_blocks, global_blocks)
     heads = queries.shape[1] // NH
-    q_s = queries.reshape(PART, NH, heads, DH).transpose(1, 0, 2, 3).reshape(NH, ROWS, DH)
-    g_s = out_grad.reshape(PART, NH, heads, DH).transpose(1, 0, 2, 3).reshape(NH, ROWS, DH)
     kv_s = jnp.stack([keys, values]).transpose(2, 0, 1, 3)
     vm = lambda shape, dtype=BF16: pltpu.VMEM(shape, dtype)
     dma = lambda *shape: pltpu.SemaphoreType.DMA(shape)
@@ -753,16 +785,17 @@
             vm((2, ROWS, DH)),
             vm((2, NY, BS, DH)), vm((2, NY, BS, DH)), vm((2, BS, DH)), vm((2, NZ, PIECE, DH)),
             vm((2, PIECE, DH)), vm((2, BS, DH)), vm((2, NY, BS, DH)),
-            dma(NH), dma(NH), dma(NH), dma(NH), dma(NH), dma(NH), dma(6),
+            vm(queries.shape),
+            dma(2, NH), dma(2, NH), dma(NH), dma(NH), dma(NH), dma(NH), dma(8),
             dma(4, 2), dma(4, 2), dma(4, 2), dma(4, 2), dma(2), dma(2), dma(8, NY), dma(8, NY),
             dma(2, NY), dma(2, NY), dma(2, NZ), dma(2, NZ), dma(2, NZ), dma(2, NZ), dma(2, NY), dma(2, NY),
             dma(NH), dma(NH), dma(NH), dma(NH), dma(8, NY), dma(8, NY), dma(2), dma(2),
-            dma(4, 2), dma(4, 2), dma(4, 2), dma(4, 2), dma(NH), dma(NH),
+            dma(4, 2), dma(4, 2), dma(4, 2), dma(4, 2), dma(2, NH), dma(2, NH),
         ],
         compiler_params=pltpu.CompilerParams(
-            collective_id=0, has_side_effects=True, vmem_limit_bytes=60 * 2**20
+            collective_id=0, has_side_effects=True, vmem_limit_bytes=62 * 2**20
         ),
-    )(tab, q_s, g_s, kv_s)
+    )(tab, queries, out_grad, kv_s)
 
     def rows_back(part):
         return part.reshape(NH, PART, heads, DH).transpose(1, 0, 2, 3).reshape(PART, NH * heads, DH)

time: 143 us -> 136 us (0.951)
  local copies, waits for them, and re-layouts: 12.2 us -> 8.91 us
  Pallas kernels: 127 us -> 125 us
    pallas_call x1, Pallas kernels: 127 us -> 125 us  [on_device(): pl.pallas_call(body, out_shape=(jax.ShapeDtypeStruct((NH, ROWS, DH), BF16...]
    reshape x1 -> x0, local copies, waits for them, and re-layouts: 2.44 us -> none  [on_device(): out_grad.reshape(PART, NH, heads, DH).transpose(1, 0, 2, 3)]
where the time goes in v4:
time: 136 us
  Pallas kernels  125 us (92%)
  local copies, waits for them, and re-layouts  8.91 us (7%)
  other arithmetic  1.82 us (1%)
    pallas_call x1, Pallas kernels, on_device(): pl.pallas_call(body, out_shape=(jax.ShapeDtypeStruct((NH, ROWS, DH), BF16...  125 us
    reshape x2, local copies, waits for them, and re-layouts, rows_back(): part.reshape(NH, PART, heads, DH).transpose(1, 0, 2, 3)  4.64 us

profile of v4, /device:TPU:1, one launch (start us, length us, event | category | flops | bytes accessed | tf_op | source)
XLA Modules:
  0.0 136.0 jit_solution(8453662629873356471)
XLA Ops:
  0.6 0.0 copy-start
  0.7 0.7 and_select_fusion.2
  1.4 0.0 copy-done
  1.4 0.1 copy.24
  1.5 0.1 reshape_reshape.3
  1.6 0.1 reshape.41
  1.8 0.2 select_reduce_fusion
  2.0 0.1 reshape.42
  2.1 0.1 select_reduce_fusion.1
  2.2 1.3 concatenate.3.tab
  3.4 1.1 copy_bitcast_fusion.2
  4.5 0.8 maximum_bitcast_fusion.kv_s
  5.3 124.5 %shard_map.93 = (bf16[8,768,128]{2,1,0:T(8,128)(2,1)}, bf16[8,768,128]{2,1,0:T(8,128)(2,1)}, bf16[8,2,96,128]{3,2,1,0:T(8,128)(2,1)}) custom-call(s32[120]{0:T(128)} %concatenate.3.tab, bf16[96,64,128]{2,1,0:T(8,128)(2,1)} %q_in.1, bf16[96,64,128]{2,1,0:T(8,128)(2,1)} %g_in.1, bf16[8,2,96,128]{3,2,1,0:T(8,128)(2,1)} %maximum_bitcast_fusion.kv_s), custom_call_target="tpu_custom_call" | custom-call | tf_op jit(solution)/shard_map/pallas_call | solution.py:761
  129.8 0.0 copy-start.2
  129.8 3.0 %copy_bitcast_fusion.1 = bf16[96,64,128]{2,1,0:T(8,128)(2,1)} fusion(bf16[8,768,128]{2,1,0:T(8,128)(2,1)} %get-tuple-element.7), kind=kLoop, calls=%fused_computation.1 | loop fusion | bytes 3145728 | tf_op jit(solution)/shard_map/reshape | solution.py:801
  132.9 0.0 copy-done.2
  132.9 0.0 copy-start.1
  132.9 0.8 copy.31
  133.7 0.8 copy.30
  134.4 0.0 copy-done.1
  134.4 1.6 %copy_bitcast_fusion = bf16[96,64,128]{2,1,0:T(8,128)(2,1)} fusion(bf16[8,768,128]{2,1,0:T(8,128)(2,1)S(1)} %copy-done.1), kind=kLoop, calls=%fused_computation | loop fusion | bytes 3145728 | tf_op jit(solution)/shard_map/reshape | solution.py:801
  (7 shorter events, 0.1 us)
Async XLA Ops:
  0.6 0.7 copy-start
  129.8 3.1 %copy-start.2 = (bf16[8,2,96,128]{3,2,1,0:T(8,128)(2,1)S(1)}, bf16[8,2,96,128]{3,2,1,0:T(8,128)(2,1)}, u32[]{:S(2)}) copy-start(bf16[8,2,96,128]{3,2,1,0:T(8,128)(2,1)} %get-tuple-element.9) | copy-start | bytes 1179652
  132.9 1.5 %copy-start.1 = (bf16[8,768,128]{2,1,0:T(8,128)(2,1)S(1)}, bf16[8,768,128]{2,1,0:T(8,128)(2,1)}, u32[]{:S(2)}) copy-start(bf16[8,768,128]{2,1,0:T(8,128)(2,1)} %get-tuple-element.8) | copy-start | bytes 4718596

commit v5 on v4

--- a/solution.py
+++ b/solution.py
@@ -35,7 +35,7 @@
 
 
 def body(
-    tab, q_in, g_in, kv_s, o_out, dq_out, dkv_out,
+    tab, q_in, g_in, kv_s, o_out, dq_out, dkv_out, o_end,
     qh, gh, r0, rp1, rp2, rp3, rm1, rm2, rm3, r4, xs, xr, edge,
     lkn, lvn, lktn, lvtn, lkf, lvf, lktf, lvtf, exn, dsf, o1, stats, ob, dqb,
     awk, awv, agk, agv, ark, arv,
@@ -476,19 +476,19 @@
     lax.fori_loop(1, NH, wait_g, 0)
 
     def o_copy(h):
-        return remote(ob.at[there_rows(h), :], o_out.at[head], o_ss.at[h], o_rs.at[head], (blk, h))
+        return remote(ob.at[there_rows(h), :], o_out.at[rows_mine, :], o_ss.at[h], o_rs.at[head], (blk, h))
 
     def dq_copy(h):
-        return remote(dqb.at[there_rows(h), :], dq_out.at[head], dq_ss.at[h], dq_rs.at[head], (blk, h))
+        return remote(dqb.at[there_rows(h), :], dq_out.at[rows_mine, :], dq_ss.at[h], dq_rs.at[head], (blk, h))
 
     def o_arrival(h):
-        return remote(ob.at[there_rows(h), :], o_out.at[h], o_ss.at[h], o_rs.at[h], (blk, h))
+        return remote(ob.at[there_rows(h), :], o_out.at[there_rows(h), :], o_ss.at[h], o_rs.at[h], (blk, h))
 
     def dq_arrival(h):
-        return remote(dqb.at[there_rows(h), :], dq_out.at[h], dq_ss.at[h], dq_rs.at[h], (blk, h))
-
-    own_o = pltpu.make_async_copy(ob.at[there_rows(head), :], o_out.at[head], loc.at[3])
-    own_dq = pltpu.make_async_copy(dqb.at[there_rows(head), :], dq_out.at[head], loc.at[4])
+        return remote(dqb.at[there_rows(h), :], dq_out.at[there_rows(h), :], dq_ss.at[h], dq_rs.at[h], (blk, h))
+
+    own_o = pltpu.make_async_copy(ob.at[there_rows(head), :], o_out.at[rows_mine, :], loc.at[3])
+    own_dq = pltpu.make_async_copy(dqb.at[there_rows(head), :], dq_out.at[rows_mine, :], loc.at[4])
 
     def far_part(n, c):
         k = NH - 1 - n
@@ -541,6 +541,25 @@
 
     def slot_rows(slot):
         return pl.ds(slot * BS, BS)
+
+    def gather_in(arrival, own, out, dst, n):
+        own.wait()
+
+        def one(k, c):
+            arrival(peer(k)).wait_recv()
+            return c
+
+        lax.fori_loop(1, NH, one, 0)
+        pltpu.make_async_copy(out, dst, loc.at[n]).start()
+
+    def gather_out(out, dst, end, n):
+        pltpu.make_async_copy(out, dst, loc.at[n]).wait()
+        for pair in range(NH // 2):
+            two = [
+                dst[h * ROWS:(h + 1) * ROWS, :].astype(F32).reshape(PART, NH, DH) for h in (2 * pair, 2 * pair + 1)
+            ]
+            raw[:, pair * 2 * NH:(pair + 1) * 2 * NH, :] = jnp.concatenate(two, axis=1).astype(BF16)
+        pltpu.make_async_copy(raw, end, loc.at[n + 1]).start()
 
     def give(index):
         sz = shard_of(back[index])
@@ -633,7 +652,9 @@
     add_up(5, partp)
     add_up(6, partm)
     pass_on(3)
+    gather_in(o_arrival, own_o, o_out, qh, 8)
     ar_three(1)
+    gather_out(o_out, qh, o_end, 8)
     add_up(7, fin)
     e2_before.wait_send()
     e2_after.wait_send()
@@ -685,6 +706,8 @@
         own_dkv(half).start()
         lax.fori_loop(1, NH, functools.partial(send_dkv, half), 0)
 
+    pltpu.make_async_copy(raw, o_end, loc.at[9]).wait()
+
     def drain(k, c):
         h = (head + k) % NH
         kv_copy(h, 0).wait_send()
@@ -693,7 +716,6 @@
         dq_copy(h).wait_send()
         dkv_copy(h, 0).wait_send()
         dkv_copy(h, 1).wait_send()
-        o_arrival(h).wait_recv()
         dq_arrival(h).wait_recv()
         dkv_arrival(h, 0).wait_recv()
         dkv_arrival(h, 1).wait_recv()
@@ -722,7 +744,6 @@
     ar_drain(0)
     ar_drain(1)
     lax.fori_loop(1, NH, drain, 0)
-    own_o.wait()
     own_dq.wait()
     own_dkv(0).wait()
     own_dkv(1).wait()
@@ -751,22 +772,22 @@
 
 def on_device(queries, keys, values, out_grad, rand_blocks, global_blocks):
     tab = tables(rand_blocks, global_blocks)
-    heads = queries.shape[1] // NH
     kv_s = jnp.stack([keys, values]).transpose(2, 0, 1, 3)
     vm = lambda shape, dtype=BF16: pltpu.VMEM(shape, dtype)
     dma = lambda *shape: pltpu.SemaphoreType.DMA(shape)
     total = NH * ROWS
     pair = (2, BS, DH)
     anywhere = pl.BlockSpec(memory_space=pl.ANY)
-    o_h, dq_h, dkv_h = pl.pallas_call(
+    _, dq_h, dkv_h, attn_out = pl.pallas_call(
         body,
         out_shape=(
-            jax.ShapeDtypeStruct((NH, ROWS, DH), BF16),
-            jax.ShapeDtypeStruct((NH, ROWS, DH), BF16),
+            jax.ShapeDtypeStruct((total, DH), BF16),
+            jax.ShapeDtypeStruct((total, DH), BF16),
             jax.ShapeDtypeStruct((NH, 2, PART, DH), BF16),
+            jax.ShapeDtypeStruct(queries.shape, BF16),
         ),
         in_specs=[pl.BlockSpec(memory_space=pltpu.SMEM), anywhere, anywhere, anywhere],
-        out_specs=(anywhere, anywhere, anywhere),
+        out_specs=(anywhere,) * 4,
         scratch_shapes=[
             vm((total, DH)), vm((total, DH)),
             *[vm((2, ROWS, DH)) for _ in range(8)],
@@ -786,7 +807,7 @@
             vm((2, NY, BS, DH)), vm((2, NY, BS, DH)), vm((2, BS, DH)), vm((2, NZ, PIECE, DH)),
             vm((2, PIECE, DH)), vm((2, BS, DH)), vm((2, NY, BS, DH)),
             vm(queries.shape),
-            dma(2, NH), dma(2, NH), dma(NH), dma(NH), dma(NH), dma(NH), dma(8),
+            dma(2, NH), dma(2, NH), dma(NH), dma(NH), dma(NH), dma(NH), dma(10),
             dma(4, 2), dma(4, 2), dma(4, 2), dma(4, 2), dma(2), dma(2), dma(8, NY), dma(8, NY),
             dma(2, NY), dma(2, NY), dma(2, NZ), dma(2, NZ), dma(2, NZ), dma(2, NZ), dma(2, NY), dma(2, NY),
             dma(NH), dma(NH), dma(NH), dma(NH), dma(8, NY), dma(8, NY), dma(2), dma(2),
@@ -797,11 +818,9 @@
         ),
     )(tab, queries, out_grad, kv_s)
 
-    def rows_back(part):
-        return part.reshape(NH, PART, heads, DH).transpose(1, 0, 2, 3).reshape(PART, NH * heads, DH)
-
+    query_grad = dq_h.reshape(NH, PART, -1, DH).transpose(1, 0, 2, 3).reshape(queries.shape)
     kv_back = dkv_h.transpose(1, 2, 0, 3)
-    return rows_back(o_h), rows_back(dq_h), kv_back[0], kv_back[1]
+    return attn_out, query_grad, kv_back[0], kv_back[1]
 
 
 def solution(mesh):

time: 136 us -> 136 us (level)
    reshape x2 -> x0, local copies, waits for them, and re-layouts: 4.64 us -> none  [rows_back(): part.reshape(NH, PART, heads, DH).transpose(1, 0, 2, 3)]
    transpose x0 -> x1, local copies, waits for them, and re-layouts: none -> 3.05 us  [on_device(): dq_h.reshape(NH, PART, -1, DH).transpose(1, 0, 2, 3).reshape(queries.shape)]
where the time goes in v5:
time: 136 us
  Pallas kernels  125 us (92%)
  local copies, waits for them, and re-layouts  8.47 us (6%)
  other arithmetic  1.82 us (1%)
    pallas_call x1, Pallas kernels, on_device(): pl.pallas_call(body, out_shape=(jax.ShapeDtypeStruct((total, DH), BF16),...  125 us
    transpose x1, local copies, waits for them, and re-layouts, on_device(): dq_h.reshape(NH, PART, -1, DH).transpose(1, 0, 2, 3).reshape(queries.shape)  3.05 us

profile of v5, /device:TPU:1, one launch (start us, length us, event | category | flops | bytes accessed | tf_op | source)
XLA Modules:
  0.0 135.6 jit_solution(5949358657957628779)
XLA Ops:
  0.6 0.0 copy-start
  0.7 0.7 and_select_fusion.2
  1.4 0.0 copy-done
  1.4 0.1 copy.22
  1.5 0.1 reshape_reshape.3
  1.6 0.1 reshape.35
  1.8 0.2 select_reduce_fusion
  2.0 0.1 reshape.36
  2.1 0.1 select_reduce_fusion.1
  2.2 1.3 concatenate.3.tab
  3.4 1.1 copy_bitcast_fusion.1
  4.5 0.8 maximum_bitcast_fusion.kv_s
  5.3 124.5 %shard_map.93 = (bf16[6144,128]{1,0:T(8,128)(2,1)}, bf16[6144,128]{1,0:T(8,128)(2,1)}, bf16[8,2,96,128]{3,2,1,0:T(8,128)(2,1)}, bf16[96,64,128]{2,1,0:T(8,128)(2,1)}) custom-call(s32[120]{0:T(128)} %concatenate.3.tab, bf16[96,64,128]{2,1,0:T(8,128)(2,1)} %q_in.1, bf16[96,64,128]{2,1,0:T(8,128)(2,1)} %g_in.1, bf16[8,2,96,128]{3,2,1,0:T(8,128)(2,1)} %maximum_bitcast_fusion.kv_s), custom_call_target="tpu_custom_call" | custom-call | tf_op jit(solution)/shard_map/pallas_call | solution.py:781
  129.8 0.0 copy-start.2
  129.9 3.0 %copy.32 = bf16[96,8,8,128]{3,2,1,0:T(8,128)(2,1)} copy(bf16[96,8,8,128]{3,2,0,1:T(8,128)(2,1)} %bitcast.30) | data formatting | bytes 3145728 | tf_op jit(solution)/shard_map/transpose | solution.py:821
  132.9 0.0 copy-start.1
  132.9 0.0 copy-done.2
  132.9 0.8 copy.28
  133.7 0.8 copy.27
  134.4 0.0 copy-done.1
  134.4 1.1 copy.34
  (7 shorter events, 0.1 us)
Async XLA Ops:
  0.6 0.7 copy-start
  129.8 3.1 %copy-start.2 = (bf16[8,2,96,128]{3,2,1,0:T(8,128)(2,1)S(1)}, bf16[8,2,96,128]{3,2,1,0:T(8,128)(2,1)}, u32[]{:S(2)}) copy-start(bf16[8,2,96,128]{3,2,1,0:T(8,128)(2,1)} %get-tuple-element.9) | copy-start | bytes 1179652
  132.9 1.5 %copy-start.1 = (bf16[96,64,128]{2,1,0:T(8,128)(2,1)S(1)}, bf16[96,64,128]{2,1,0:T(8,128)(2,1)}, u32[]{:S(2)}) copy-start(bf16[96,64,128]{2,1,0:T(8,128)(2,1)} %get-tuple-element.37) | copy-start | bytes 4718596
